TPU v7x, 32 devices: a whole 2x2x4 slice. The times are simulated.
32 devices in a mesh: dp: 16 (over z, y, x), pair: 2 (over core).
Axes of the slice: x: 2, y: 2, z: 4, core: 2. Of those that a mesh axis runs over, the one named last changes fastest.
Arguments:
- text_inputs: bfloat16 [8192, 768], P(('dp', 'pair')), may hold values from -6 to 6
- region_features: bfloat16 [8192, 2048], P(('dp', 'pair')), may hold values from -6 to 6
- text_masked: int32 [8192], P(('dp', 'pair')), may hold values 0 or 1
- region_masked: int32 [8192], P(('dp', 'pair')), may hold values 0 or 1
- text_anchors: int32 [2, 8192], P(None, ('dp', 'pair')), may hold values from 0 to 1023
- region_anchors: int32 [2, 8192], P(None, ('dp', 'pair')), may hold values from 0 to 1023
- backbone_weight: bfloat16 [2048, 768], P(('dp', 'pair')), may hold values from -0.125 to 0.125
- batch_gain: bfloat16 [768], P(('dp', 'pair')), may hold values from 0.5 to 1.5
- batch_shift: bfloat16 [768], P(('dp', 'pair')), may hold values from -4 to 4
- text_blank: bfloat16 [768], P(('dp', 'pair')), may hold values from -6 to 6
- region_blank: bfloat16 [768], P(('dp', 'pair')), may hold values from -6 to 6
- position_table: bfloat16 [1024, 1536], P(('dp', 'pair')), may hold values from -6 to 6
- stream_weights: bfloat16 [768, 7680], P(('dp', 'pair')), may hold values from -0.21875 to 0.21875
- linear_bias: bfloat16 [256, 12], P(('dp', 'pair')), may hold values from -6 to 6
- planar_bias: bfloat16 [256, 12], P(('dp', 'pair')), may hold values from -6 to 6
- merge_weight: bfloat16 [768, 768], P(('dp', 'pair')), may hold values from -1.75 to 1.75
- mixer_gain: bfloat16 [768], P(('dp', 'pair')), may hold values from 0.5 to 1.5
- mixer_shift: bfloat16 [768], P(('dp', 'pair')), may hold values from -4 to 4
- expand_weight: bfloat16 [768, 3072], P(('dp', 'pair')), may hold values from -0.21875 to 0.21875
- expand_bias: bfloat16 [3072], P(('dp', 'pair')), may hold values from -4 to 4
- reduce_weight: bfloat16 [3072, 768], P(('dp', 'pair')), may hold values from -0.109375 to 0.109375
- reduce_bias: bfloat16 [768], P(('dp', 'pair')), may hold values from -4 to 4
- output_gain: bfloat16 [768], P(('dp', 'pair')), may hold values from 0.5 to 1.5
- output_shift: bfloat16 [768], P(('dp', 'pair')), may hold values from -4 to 4
- cotangent: bfloat16 [8192, 768], P(('dp', 'pair')), may hold values from -6 to 6
Outputs:
- layer_output: bfloat16 [8192, 768], P(('dp', 'pair'))
- text_gradient: float32 [8192, 768], P(('dp', 'pair'))
- feature_gradient: float32 [8192, 2048], P(('dp', 'pair'))
- backbone_weight_gradient: float32 [2048, 768], P(('dp', 'pair'))
- batch_gain_gradient: float32 [768], P(('dp', 'pair'))
- batch_shift_gradient: float32 [768], P(('dp', 'pair'))
- text_blank_gradient: float32 [768], P(('dp', 'pair'))
- region_blank_gradient: float32 [768], P(('dp', 'pair'))
- position_table_gradient: float32 [1024, 1536], P(('dp', 'pair'))
- stream_weights_gradient: float32 [768, 7680], P(('dp', 'pair'))
- linear_bias_gradient: float32 [256, 12], P(('dp', 'pair'))
- planar_bias_gradient: float32 [256, 12], P(('dp', 'pair'))
- merge_weight_gradient: float32 [768, 768], P(('dp', 'pair'))
- mixer_gain_gradient: float32 [768], P(('dp', 'pair'))
- mixer_shift_gradient: float32 [768], P(('dp', 'pair'))
- expand_weight_gradient: float32 [768, 3072], P(('dp', 'pair'))
- expand_bias_gradient: float32 [3072], P(('dp', 'pair'))
- reduce_weight_gradient: float32 [3072, 768], P(('dp', 'pair'))
- reduce_bias_gradient: float32 [768], P(('dp', 'pair'))
- output_gain_gradient: float32 [768], P(('dp', 'pair'))
- output_shift_gradient: float32 [768], P(('dp', 'pair'))
All inputs are finite; a program needn't handle non-finite values. No bound on the sum of `text_masked` or of `region_masked` on one device may be relied on, other than what follows from the above.
Results may differ from a plain program's by a relative error of at most 0.017.
Values may be sent and summed in bfloat16 or wider, within the bound.
A program may use at most 320 MiB of HBM per device.

v0:
```python
from functools import partial
from types import SimpleNamespace

import jax
import jax.numpy as jnp
from jax import lax
from jax.experimental import pallas as pl
from jax.experimental.pallas import tpu as pltpu
from jax.sharding import PartitionSpec as P

HEADS = 12
HEAD_DIM = 64
COORDS = 1024
REL_B = 256
SP_SIDE = 16
PAGE_TOKENS = 256
MODEL_WIDTH = 768
SP_B = 256
COORD_STEP = 128
PAIRS = HEADS // 2
LANES = 2 * HEAD_DIM


def dot_nt(left, right):
    return lax.dot_general(left, right, (((1,), (1,)), ((), ())), preferred_element_type=jnp.float32)


def dot_tn(left, right):
    return lax.dot_general(left, right, (((0,), (0,)), ((), ())), preferred_element_type=jnp.float32)


def dot_nn(left, right):
    return lax.dot_general(left, right, (((1,), (0,)), ((), ())), preferred_element_type=jnp.float32)


def head_columns(stream, kind, pair):
    return pl.ds(pl.multiple_of(((5 * stream + kind) * PAIRS + pair) * LANES, LANES), LANES)


def make_boxes(rows_ref, cols_ref, box_ref):
    for stream in range(2):
        part = []
        for axis in range(2):
            along = rows_ref[2 * stream + axis : 2 * stream + axis + 1, :]
            down = cols_ref[:, 2 * stream + axis : 2 * stream + axis + 1]
            part.append(((along - down) >> 7) + SP_SIDE // 2)
        box_ref[stream] = part[0] * SP_SIDE + part[1]


def attend_pair(pair, proj_ref, linear_ref, planar_ref, box_ref, merged_ref, probs_ref):
    lane_head = lax.broadcasted_iota(jnp.int32, (PAGE_TOKENS, LANES), 1) // HEAD_DIM
    mixed = [None, None]
    for inner in range(2):
        head = 2 * pair + inner
        mine = lane_head == inner
        spread = jnp.broadcast_to(linear_ref[head], (PAGE_TOKENS, 2 * PAGE_TOKENS))
        linear_term = pltpu.roll(spread, PAGE_TOKENS + 1, 1, stride=1, stride_axis=0)[:, :PAGE_TOKENS]
        low_table = jnp.broadcast_to(planar_ref[head, :, :128], (PAGE_TOKENS, 128))
        high_table = jnp.broadcast_to(planar_ref[head, :, 128:], (PAGE_TOKENS, 128))
        total = None
        for stream in range(2):
            pieces = [proj_ref[:, head_columns(stream, kind, pair)] for kind in range(5)]
            zero = jnp.zeros_like(pieces[0])
            left = jnp.concatenate([jnp.where(mine, pieces[0], zero), jnp.where(mine, pieces[3], zero)], axis=1)
            right = jnp.concatenate([pieces[1], pieces[4]], axis=1)
            logits = dot_nt(left, right) * HEAD_DIM ** (-0.5)
            planar = []
            for half in range(2):
                box = box_ref[stream, :, 128 * half : 128 * half + 128]
                place = box & 127
                planar.append(
                    jnp.where(
                        box < 128,
                        jnp.take_along_axis(low_table, place, axis=1),
                        jnp.take_along_axis(high_table, place, axis=1),
                    )
                )
            logits = logits + linear_term + jnp.concatenate(planar, axis=1)
            top = jnp.max(logits, axis=-1, keepdims=True)
            shifted = jnp.exp(logits - top)
            probs = shifted / jnp.sum(shifted, axis=-1, keepdims=True)
            probs_ref[stream, inner] = probs
            part = dot_nn(probs.astype(jnp.bfloat16), pieces[2])
            total = part if total is None else total + part
        mixed[inner] = total
    merged_ref[...] = jnp.where(lane_head == 0, mixed[0], mixed[1]).astype(jnp.bfloat16)


def make_places(rows_ref, cols_ref, place_ref, turned_ref, mask_ref, flip_ref):
    lanes = lax.broadcasted_iota(jnp.int32, (PAGE_TOKENS, SP_B), 1)
    rows = lax.broadcasted_iota(jnp.int32, (PAGE_TOKENS, SP_B), 0)
    flip_ref[...] = (lanes + rows == PAGE_TOKENS - 1).astype(jnp.bfloat16)
    for stream in range(2):
        x_row = rows_ref[2 * stream : 2 * stream + 1, :]
        y_row = rows_ref[2 * stream + 1 : 2 * stream + 2, :]
        x_col = cols_ref[:, 2 * stream : 2 * stream + 1]
        y_col = cols_ref[:, 2 * stream + 1 : 2 * stream + 2]
        cell_row = (x_row >> 7) * SP_SIDE + (y_row >> 7)
        cell_col = (x_col >> 7) * SP_SIDE + (y_col >> 7)
        x_less = ((x_row & 127) < (x_col & 127)).astype(jnp.float32)
        y_less = ((y_row & 127) < (y_col & 127)).astype(jnp.float32)
        for x_side in range(2):
            for y_side in range(2):
                side = 2 * x_side + y_side
                place_ref[stream, side * PAGE_TOKENS : (side + 1) * PAGE_TOKENS, :] = (
                    lanes == cell_col + (SP_SIDE + 1 - SP_SIDE * x_side - y_side)
                ).astype(jnp.bfloat16)
                mask_ref[stream, side] = (
                    (x_less if x_side else 1.0 - x_less) * (y_less if y_side else 1.0 - y_less)
                ).astype(jnp.bfloat16)
        turned_ref[stream] = (rows[:128] == 127 - cell_row).astype(jnp.bfloat16)


def attend_back_pair(
    pair, pump, proj_ref, probs_ref, upstream_ref, grad_ref, linear_ref, planar_ref,
    place_ref, turned_ref, mask_ref, flip_ref,
):
    lane_head = lax.broadcasted_iota(jnp.int32, (PAGE_TOKENS, LANES), 1) // HEAD_DIM
    wide_head = jnp.concatenate([lane_head, lane_head], axis=1)
    upstream = upstream_ref[...]
    scale = HEAD_DIM ** (-0.5)
    diagonal = [None, None]
    for stream in range(2):
        pieces = [proj_ref[:, head_columns(stream, kind, pair)] for kind in range(5)]
        queries = jnp.concatenate([pieces[0], pieces[3]], axis=1)
        keys = jnp.concatenate([pieces[1], pieces[4]], axis=1)
        grads = []
        for inner in range(2):
            head = 2 * pair + inner
            mine = lane_head == inner
            grad_probs = dot_nt(jnp.where(mine, upstream, jnp.zeros_like(upstream)), pieces[2])
            probs = probs_ref[stream, inner]
            weighted = probs * grad_probs
            grad_logits = (weighted - probs * jnp.sum(weighted, axis=-1, keepdims=True)).astype(jnp.bfloat16)
            grads.append(
                (
                    dot_nn(grad_logits, keys) * scale,
                    dot_tn(grad_logits, queries) * scale,
                    dot_tn(probs.astype(jnp.bfloat16), upstream),
                )
            )
            parts = jnp.concatenate([grad_logits * mask_ref[stream, side] for side in range(4)], axis=1)
            placed = dot_nn(parts, place_ref[stream])
            placed_high = placed.astype(jnp.bfloat16)
            placed_low = (placed - placed_high.astype(jnp.float32)).astype(jnp.bfloat16)
            turned = turned_ref[stream]
            cells = dot_nn(turned, placed_high) + dot_nn(turned, placed_low)
            sums = jnp.sum(
                pltpu.roll(cells, SP_B - SP_SIDE // 2, 1, stride=1, stride_axis=0), axis=0, keepdims=True
            )
            if stream == 0:
                planar_ref[head] = sums
            else:
                planar_ref[head] += sums
            turned_over = dot_nn(flip_ref[...], grad_logits)
            diagonal[inner] = turned_over if stream == 0 else diagonal[inner] + turned_over
            pump(2 * stream + inner)
        query_grad, key_grad = (jnp.where(wide_head == 0, grads[0][k], grads[1][k]) for k in range(2))
        value_grad = jnp.where(lane_head == 0, grads[0][2], grads[1][2])
        for kind, value in enumerate(
            (query_grad[:, :LANES], key_grad[:, :LANES], value_grad, query_grad[:, LANES:], key_grad[:, LANES:])
        ):
            grad_ref[:, head_columns(stream, kind, pair)] = value.astype(jnp.bfloat16)
    for inner in range(2):
        padded = jnp.concatenate([diagonal[inner], jnp.zeros_like(diagonal[inner])], axis=1)
        linear_ref[2 * pair + inner] = jnp.sum(
            pltpu.roll(padded, 0, 1, stride=1, stride_axis=0), axis=0, keepdims=True
        )


def linear_extended(linear_bias):
    rows = linear_bias.astype(jnp.float32).T
    low = jnp.broadcast_to(rows[:, :1], (HEADS, PAGE_TOKENS - 1 - REL_B // 2))
    high = jnp.broadcast_to(rows[:, -1:], (HEADS, PAGE_TOKENS - REL_B // 2 + 1))
    return jnp.concatenate([low, rows, high], axis=1)[:, None, :]


def linear_folded(sums):
    first = REL_B // 2
    last = PAGE_TOKENS - 1 + REL_B // 2 - 1
    return jnp.concatenate(
        [
            jnp.sum(sums[:, :first], axis=1, keepdims=True),
            sums[:, first:last],
            jnp.sum(sums[:, last : 2 * PAGE_TOKENS - 1], axis=1, keepdims=True),
        ],
        axis=1,
    )


MESH = pl.DeviceIdType.MESH
RING = 4


def place():
    dp = lax.axis_index("dp")
    return dp // RING, lax.rem(dp, RING), lax.axis_index("pair")


def across(q, bit):
    other = lax.rem(q // bit, 2)
    return q + bit - 2 * bit * other


def greet(line):
    z, q, c = place()
    barrier = pltpu.get_barrier_semaphore()

    def signal(zz, qq, cc):
        pl.semaphore_signal(barrier, inc=1, device_id={"dp": zz * RING + qq, "pair": cc}, device_id_type=MESH)

    signal(z, across(q, 1), c)
    signal(z, across(q, 2), c)
    signal(z, q, 1 - c)

    @pl.when(z > 0)
    def _():
        signal(z - 1, q, c)

    @pl.when(z < line - 1)
    def _():
        signal(z + 1, q, c)

    ends = (z > 0).astype(jnp.int32) + (z < line - 1).astype(jnp.int32)
    pl.semaphore_wait(barrier, 3 + ends)


def spread(line, pumps, pump, first, work):
    total = line - first
    low, high = (first + total * (pump + k) // pumps for k in range(2))
    if high == low + 1:
        work(low)
    elif high > low:
        lax.fori_loop(low, high, lambda g, unused: (work(g), unused)[1], 0)


def gather_stages(line, ins, outs, sems):
    count = len(ins)
    (own_sem, z_send, z_recv, xy_send, xy_recv, d_send, d_recv, c_send, c_recv) = sems
    z, q, c = place()
    beside = (across(q, 1), across(q, 2))
    corner = across(across(q, 1), 2)

    def slot(zz, qq):
        return (zz * RING + qq) * 2 + c

    def remote(src, dst, send, recv, zz, qq, cc):
        return pltpu.make_async_remote_copy(
            src_ref=src, dst_ref=dst, send_sem=send, recv_sem=recv,
            device_id={"dp": zz * RING + qq, "pair": cc}, device_id_type=MESH,
        )

    def block(a, zz, qq):
        return outs[a].at[slot(zz, qq)]

    def halves(a):
        width = ins[a].shape[-1]
        cut = width // 2 if width % 256 == 0 else width
        return (0, cut), (cut, width - cut)

    def own(a):
        return pltpu.make_async_copy(ins[a], block(a, z, q), own_sem.at[a])

    def z_copy(a, way, step, first):
        zz = z - step if way == 0 else z + step
        target = z + 1 if way == 0 else z - 1
        src = ins[a] if first else block(a, zz, q)
        return remote(src, block(a, zz, q), z_send.at[way, a, step], z_recv.at[way, a, step], target, q, c)

    def xy_copy(a, axis, zz, first):
        src = ins[a] if first else block(a, zz, q)
        return remote(src, block(a, zz, q), xy_send.at[axis, a, zz], xy_recv.at[axis, a, zz], z, beside[axis], c)

    def d_copy(a, axis, zz):
        start, width = halves(a)[axis]
        part = outs[a].at[slot(zz, beside[axis]), :, pl.ds(start, width)]
        return remote(part, part, d_send.at[axis, a, zz], d_recv.at[axis, a, zz], z, beside[1 - axis], c)

    def c_copy(a, zz, qq, first):
        src = ins[a] if first else block(a, zz, qq)
        return remote(
            src, block(a, zz, qq), c_send.at[a, zz * RING + qq], c_recv.at[a, zz * RING + qq], z, q, 1 - c
        )

    def start():
        for a in range(count):
            own(a).start()
            for way in range(2):
                @pl.when(z < line - 1 if way == 0 else z > 0)
                def _():
                    z_copy(a, way, 0, True).start()
            for axis in range(2):
                xy_copy(a, axis, z, True).start()
            c_copy(a, z, q, True).start()

    def arrived(a, zz):
        for axis in range(2):
            xy_copy(a, axis, zz, False).start()
        c_copy(a, zz, q, False).start()

    def passed_on(a, zz):
        for axis in range(2):
            start, width = halves(a)[axis]
            got = block(a, zz, beside[axis])
            remote(got, got, xy_send.at[axis, a, zz], xy_recv.at[axis, a, zz], z, beside[axis], c).wait_recv()
            if width:
                d_copy(a, axis, zz).start()
            c_copy(a, zz, beside[axis], False).start()

    def finished(a, zz):
        for axis in range(2):
            start, width = halves(a)[axis]
            if width:
                part = outs[a].at[slot(zz, corner), :, pl.ds(start, width)]
                remote(part, part, d_send.at[axis, a, zz], d_recv.at[axis, a, zz], z, beside[1 - axis], c).wait_recv()
        c_copy(a, zz, corner, False).start()

    def both_ways(g, work):
        @pl.when(z - g >= 0)
        def _():
            work(z - g)

        @pl.when(jnp.logical_and(z + g <= line - 1, g > 0))
        def _():
            work(z + g)

    def along(g):
        for a in range(count):
            @pl.when(z - g >= 0)
            def _():
                got = block(a, z - g, q)
                remote(got, got, z_send.at[0, a, g - 1], z_recv.at[0, a, g - 1], z, q, 1 - c).wait_recv()

                @pl.when(z < line - 1)
                def _():
                    z_copy(a, 0, g, False).start()

                arrived(a, z - g)

            @pl.when(z + g <= line - 1)
            def _():
                got = block(a, z + g, q)
                remote(got, got, z_send.at[1, a, g - 1], z_recv.at[1, a, g - 1], z, q, 1 - c).wait_recv()

                @pl.when(z > 0)
                def _():
                    z_copy(a, 1, g, False).start()

                arrived(a, z + g)

    def around(g):
        for a in range(count):
            both_ways(g, partial(passed_on, a))

    def home(g):
        for a in range(count):
            both_ways(g, partial(finished, a))

    def drain(zz, unused):
        for a in range(count):
            for axis in range(2):
                xy_copy(a, axis, zz, False).wait_send()
                if halves(a)[axis][1]:
                    d_copy(a, axis, zz).wait_send()
            for qq in range(RING):
                c_copy(a, zz, qq, False).wait_send()
                got = outs[a].at[(zz * RING + qq) * 2 + 1 - c]
                remote(
                    got, got, c_send.at[a, zz * RING + qq], c_recv.at[a, zz * RING + qq], z, q, 1 - c
                ).wait_recv()

            @pl.when(jnp.logical_and(z < line - 1, zz <= z))
            def _():
                z_copy(a, 0, z - zz, False).wait_send()

            @pl.when(jnp.logical_and(z > 0, zz >= z))
            def _():
                z_copy(a, 1, zz - z, False).wait_send()
        return unused

    def end():
        for a in range(count):
            own(a).wait()
        lax.fori_loop(0, line, drain, 0)

    return SimpleNamespace(start=start, along=along, around=around, home=home, end=end)


def gather_sems(line, count):
    dma = pltpu.SemaphoreType.DMA
    return [
        dma((count,)),
        *(dma((2, count, line)) for k in range(6)),
        dma((count, line * RING)),
        dma((count, line * RING)),
    ]


def gather_kernel(line, count, *refs):
    stages = gather_stages(line, refs[:count], refs[count : 2 * count], refs[2 * count :])
    greet(line)
    stages.start()

    def generation(g, unused):
        @pl.when(g <= line - 1)
        def _():
            stages.along(g)

        @pl.when(g <= line)
        def _():
            stages.around(g - 1)

        @pl.when(g >= 2)
        def _():
            stages.home(g - 2)

        return unused

    lax.fori_loop(1, line + 2, generation, 0)
    stages.end()


def gather_all(shards, collective_id):
    dp = lax.axis_size("dp")
    line = dp // RING
    devices = 2 * dp
    count = len(shards)
    return pl.pallas_call(
        partial(gather_kernel, line, count),
        in_specs=[pl.BlockSpec(memory_space=pl.ANY)] * count,
        out_specs=[pl.BlockSpec(memory_space=pl.ANY)] * count,
        out_shape=[jax.ShapeDtypeStruct((devices, *shard.shape), shard.dtype) for shard in shards],
        scratch_shapes=gather_sems(line, count),
        compiler_params=pltpu.CompilerParams(collective_id=collective_id, has_side_effects=True),
        name="gather_all",
    )(*shards)


def scatter_stages(line, ins, outs, scratch):
    count = len(ins)
    groups = [scratch[k * count : (k + 1) * count] for k in range(5)]
    mine, beside_sum, half_in, full_in, line_in = groups
    (own_sem, c_send, c_recv, d_send, d_recv, xy_send, xy_recv, z_send, z_recv) = scratch[5 * count :]
    z, q, c = place()
    beside = (across(q, 1), across(q, 2))
    corner = across(across(q, 1), 2)

    def remote(src, dst, send, recv, zz, qq, cc):
        return pltpu.make_async_remote_copy(
            src_ref=src, dst_ref=dst, send_sem=send, recv_sem=recv,
            device_id={"dp": zz * RING + qq, "pair": cc}, device_id_type=MESH,
        )

    def halves(a):
        width = outs[a].shape[-1]
        cut = width // 2 if width % 256 == 0 else width
        return (0, cut), (cut, width - cut)

    def wide(value):
        return value.astype(jnp.float32)

    def group(zz):
        return pl.ds(zz * RING, RING)

    def own(a, zz):
        return pltpu.make_async_copy(ins[a].at[group(zz), c], mine[a].at[group(zz)], own_sem.at[a, zz])

    def c_copy(a, zz):
        return remote(
            ins[a].at[group(zz), 1 - c], beside_sum[a].at[group(zz)], c_send.at[a, zz], c_recv.at[a, zz], z, q, 1 - c
        )

    def d_copy(a, axis, zz):
        start, width = halves(a)[axis]
        return remote(
            mine[a].at[zz * RING + corner, :, pl.ds(start, width)],
            half_in[a].at[zz, :, pl.ds(start, width)],
            d_send.at[axis, a, zz], d_recv.at[axis, a, zz], z, beside[axis], c,
        )

    def xy_copy(a, axis, zz):
        return remote(
            mine[a].at[zz * RING + beside[axis]], full_in[a].at[axis, zz],
            xy_send.at[axis, a, zz], xy_recv.at[axis, a, zz], z, beside[axis], c,
        )

    def z_copy(a, way, zz):
        return remote(
            mine[a].at[zz * RING + q], line_in[a].at[way, zz],
            z_send.at[way, a, zz], z_recv.at[way, a, zz], z + 1 if way == 0 else z - 1, q, c,
        )

    def both_ways(g, work):
        @pl.when(z - g >= 0)
        def _():
            work(z - g)

        @pl.when(jnp.logical_and(z + g <= line - 1, g > 0))
        def _():
            work(z + g)

    def begin(zz):
        for a in range(count):
            c_copy(a, zz).start()
            own(a, zz).start()

    def first(zz):
        for a in range(count):
            own(a, zz).wait()
            c_copy(a, zz).wait_recv()

            def one(qq, unused):
                k = zz * RING + qq
                mine[a][k] = mine[a][k] + beside_sum[a][k]
                return unused

            lax.fori_loop(0, RING, one, 0)
            for axis in range(2):
                if halves(a)[axis][1]:
                    d_copy(a, axis, zz).start()

    def second(zz):
        for a in range(count):
            for axis in range(2):
                start, width = halves(a)[axis]
                k = zz * RING + beside[1 - axis]
                if width:
                    d_copy(a, axis, zz).wait_recv()
                    mine[a][k, :, start : start + width] = (
                        mine[a][k, :, start : start + width] + half_in[a][zz, :, start : start + width]
                    )
                xy_copy(a, 1 - axis, zz).start()

    def third(zz):
        for a in range(count):
            k = zz * RING + q
            for axis in range(2):
                xy_copy(a, axis, zz).wait_recv()
            mine[a][k] = (
                wide(mine[a][k]) + wide(full_in[a][0, zz]) + wide(full_in[a][1, zz])
            ).astype(mine[a].dtype)
            for way in range(2):
                @pl.when(zz > z if way == 0 else zz < z)
                def _():
                    @pl.when(z > 0 if way == 0 else z < line - 1)
                    def _():
                        z_copy(a, way, zz).wait_recv()
                        mine[a][k] = mine[a][k] + line_in[a][way, zz]

                    z_copy(a, way, zz).start()

            @pl.when(zz == z)
            def _():
                outs[a][...] = wide(mine[a][k])
                for way in range(2):
                    @pl.when(z > 0 if way == 0 else z < line - 1)
                    def _():
                        z_copy(a, way, zz).wait_recv()
                        outs[a][...] += wide(line_in[a][way, zz])

    def start():
        def begin_all(step, unused):
            both_ways(line - 1 - step, begin)
            return unused

        lax.fori_loop(0, line, begin_all, 0)

    def drain(zz, unused):
        for a in range(count):
            for axis in range(2):
                xy_copy(a, axis, zz).wait_send()
                if halves(a)[axis][1]:
                    d_copy(a, axis, zz).wait_send()
            c_copy(a, zz).wait_send()
            for way in range(2):
                @pl.when(zz > z if way == 0 else zz < z)
                def _():
                    z_copy(a, way, zz).wait_send()
        return unused

    def end():
        lax.fori_loop(0, line, drain, 0)

    return SimpleNamespace(
        start=start,
        first=lambda step: both_ways(line - 1 - step, first),
        second=lambda step: both_ways(line - 1 - step, second),
        third=lambda step: both_ways(line - 1 - step, third),
        end=end,
    )


def scatter_scratch(line, blocks):
    dma = pltpu.SemaphoreType.DMA
    count = len(blocks)
    return [
        *(pltpu.VMEM((line * RING, *shape), kind) for shape, kind in blocks),
        *(pltpu.VMEM((line * RING, *shape), kind) for shape, kind in blocks),
        *(pltpu.VMEM((line, *shape), kind) for shape, kind in blocks),
        *(pltpu.VMEM((2, line, *shape), kind) for shape, kind in blocks),
        *(pltpu.VMEM((2, line, *shape), kind) for shape, kind in blocks),
        *(dma((count, line)) for k in range(3)),
        *(dma((2, count, line)) for k in range(6)),
    ]


def scatter_kernel(line, count, *refs):
    stages = scatter_stages(line, refs[:count], refs[count : 2 * count], refs[2 * count :])
    greet(line)
    stages.start()

    def generation(step, unused):
        @pl.when(step < line)
        def _():
            stages.first(step)

        @pl.when(jnp.logical_and(step >= 1, step <= line))
        def _():
            stages.second(step - 1)

        @pl.when(step >= 2)
        def _():
            stages.third(step - 2)

        return unused

    lax.fori_loop(0, line + 2, generation, 0)
    stages.end()


def scatter_all(grads, collective_id):
    dp = lax.axis_size("dp")
    line = dp // RING
    count = len(grads)
    blocks = [(grad.shape[1:], grad.dtype) for grad in grads]
    return pl.pallas_call(
        partial(scatter_kernel, line, count),
        in_specs=[pl.BlockSpec(memory_space=pl.ANY)] * count,
        out_specs=[pl.BlockSpec(memory_space=pltpu.VMEM)] * count,
        out_shape=[jax.ShapeDtypeStruct(shape, jnp.float32) for shape, kind in blocks],
        scratch_shapes=scatter_scratch(line, blocks),
        compiler_params=pltpu.CompilerParams(
            collective_id=collective_id, has_side_effects=True, vmem_limit_bytes=63 << 20
        ),
        name="scatter_all",
    )(*(grad.reshape(line * RING, 2, *grad.shape[1:]) for grad in grads))


def peers(line):
    z, q, c = place()
    cell = q * 2 + c
    near = RING * 2

    def near_place(k):
        other = lax.rem(cell + k, near)
        return other, {"dp": z * RING + other // 2, "pair": lax.rem(other, 2)}

    def far_place(k):
        other = lax.rem(z + k, line)
        return other, {"dp": other * RING + q, "pair": c}

    def each(places, stop, work):
        def one(k, unused):
            work(*places(k))
            return unused

        lax.fori_loop(1, stop, one, 0)

    return partial(each, near_place, near), partial(each, far_place, line)


def greet_peers(line):
    barrier = pltpu.get_barrier_semaphore()
    for each in peers(line):
        each(
            lambda other, device: pl.semaphore_signal(barrier, inc=1, device_id=device, device_id_type=MESH)
        )
    pl.semaphore_wait(barrier, 2 * RING + line - 2)


def exchange_stages(line, combine, value_ref, total_ref, scratch):
    near_ref, part_ref, far_ref, n_send, n_recv, f_send, f_recv = scratch
    z, q, c = place()
    cell = q * 2 + c
    each_near, each_far = peers(line)

    def near_copy(other, device, source):
        return pltpu.make_async_remote_copy(
            src_ref=value_ref, dst_ref=near_ref.at[source], send_sem=n_send.at[other], recv_sem=n_recv.at[source],
            device_id=device, device_id_type=MESH,
        )

    def far_copy(other, device, source):
        return pltpu.make_async_remote_copy(
            src_ref=part_ref, dst_ref=far_ref.at[source], send_sem=f_send.at[other], recv_sem=f_recv.at[source],
            device_id=device, device_id_type=MESH,
        )

    def near():
        each_near(lambda other, device: near_copy(other, device, cell).start())
        near_ref[cell] = value_ref[...]

    def far():
        each_near(lambda other, device: near_copy(other, device, other).wait_recv())
        part_ref[...] = combine(near_ref, 2 * RING, 1)
        each_far(lambda other, device: far_copy(other, device, z).start())
        far_ref[z] = part_ref[...]

    def total():
        each_far(lambda other, device: far_copy(other, device, other).wait_recv())
        total_ref[...] = combine(far_ref, line, 2 * RING)

    def end():
        each_near(lambda other, device: near_copy(other, device, cell).wait_send())
        each_far(lambda other, device: far_copy(other, device, z).wait_send())

    return SimpleNamespace(near=near, far=far, total=total, end=end)


def exchange_scratch(line, shape):
    dma = pltpu.SemaphoreType.DMA
    near = 2 * RING
    return [
        pltpu.VMEM((near, *shape), jnp.float32),
        pltpu.VMEM(shape, jnp.float32),
        pltpu.VMEM((line, *shape), jnp.float32),
        dma((near,)),
        dma((near,)),
        dma((line,)),
        dma((line,)),
    ]


def exchange_kernel(line, combine, value_ref, total_ref, *scratch):
    stages = exchange_stages(line, combine, value_ref, total_ref, scratch)
    greet_peers(line)
    stages.near()
    stages.far()
    stages.total()
    stages.end()


def add_up(parts, count, weight):
    return lax.fori_loop(1, count, lambda k, total: total + parts[k], parts[0])


def pool_statistics(rows, parts, count, weight):
    mean = lax.fori_loop(1, count, lambda k, total: total + parts[k, 0], parts[0, 0]) / count

    def squares(k, total):
        offset = parts[k, 0] - mean
        return total + parts[k, 1] + (rows * weight) * (offset * offset)

    return jnp.stack([mean, lax.fori_loop(0, count, squares, jnp.zeros_like(mean))])


def exchange(value, combine, collective_id, name):
    line = lax.axis_size("dp") // RING
    vmem = pl.BlockSpec(memory_space=pltpu.VMEM)
    return pl.pallas_call(
        partial(exchange_kernel, line, combine),
        in_specs=[vmem],
        out_specs=vmem,
        out_shape=jax.ShapeDtypeStruct(value.shape, value.dtype),
        scratch_shapes=exchange_scratch(line, value.shape),
        compiler_params=pltpu.CompilerParams(collective_id=collective_id, has_side_effects=True),
        name=name,
    )(value)


KINDS = 10


def source_of(column):
    stream = column // 5
    return 2 * stream + (column - 5 * stream) // 3


def once(shape):
    return pl.BlockSpec(shape, lambda i: (0,) * len(shape), pipeline_mode=pl.Buffered(1))


def at_steps(schedule):
    step = pl.program_id(0)
    for when, work in schedule:
        @pl.when(step == when)
        def _():
            for one in work:
                one()


batch_epsilon = 1e-05


def column_at_step(step):
    turn = jnp.clip(step - 1, 0, KINDS - 1)
    return jnp.where(turn >= 7, turn - 2, jnp.where(turn >= 5, turn + 3, turn))


def forward_kernel(line, count, token_total, *refs):
    (
        features_ref, backbone_ref, table_ref, text_ref, hits_ref, vectors_ref, weight_ref, linear_ref, planar_ref,
        rows_ref, cols_ref,
    ) = refs[:11]
    ins = refs[11 : 11 + count]
    proj_ref, merged_ref, probs_ref, lefts_ref, start_ref, normal_ref, scale_ref = refs[11 + count : 18 + count]
    outs = refs[18 + count : 18 + 2 * count]
    box_ref, conv_ref, local_ref, pooled_ref = refs[18 + 2 * count : 22 + 2 * count]
    rest = refs[22 + 2 * count :]
    rows = features_ref.shape[0]
    sums = exchange_stages(line, partial(pool_statistics, float(rows)), local_ref, pooled_ref, rest[:7])
    stages = gather_stages(line, ins, outs, rest[7:])
    step = pl.program_id(0)

    def vector(k):
        return vectors_ref[k : k + 1, :]

    def hit_rows(stream):
        return jnp.broadcast_to(hits_ref[:, stream : stream + 1] == 1, (rows, MODEL_WIDTH))

    @pl.when(step == 0)
    def _():
        greet_peers(line)
        conv = dot_nn(features_ref[...], backbone_ref[...])
        mean = jnp.mean(conv, axis=0, keepdims=True)
        center = conv - mean
        conv_ref[...] = conv
        local_ref[0] = mean
        local_ref[1] = jnp.sum(center * center, axis=0, keepdims=True)
        sums.near()
        stages.start()
        make_boxes(rows_ref, cols_ref, box_ref)
        text_start = jnp.where(hit_rows(0), vector(2), text_ref[...].astype(jnp.float32))
        start_ref[...] = text_start
        lefts_ref[0] = text_start.astype(jnp.bfloat16)
        coords = lax.broadcasted_iota(jnp.int32, (rows, COORDS), 1)
        for stream in range(2):
            space = None
            for axis in range(2):
                place = 2 * stream + axis
                hit = (coords == cols_ref[:, place : place + 1]).astype(jnp.bfloat16)
                part = dot_nn(hit, table_ref[:, axis * MODEL_WIDTH : (axis + 1) * MODEL_WIDTH])
                space = part if space is None else space + part
            lefts_ref[2 * stream + 1] = space.astype(jnp.bfloat16)
        sums.far()

    @pl.when(jnp.logical_and(step >= 1, step <= KINDS))
    def _():
        column = column_at_step(step)
        columns = pl.ds(pl.multiple_of(column * MODEL_WIDTH, MODEL_WIDTH), MODEL_WIDTH)
        proj_ref[:, columns] = dot_nn(lefts_ref[source_of(column)], weight_ref[...]).astype(jnp.bfloat16)

    @pl.when(step == 7)
    def _():
        sums.total()
        inverse = lax.rsqrt(pooled_ref[1] / token_total + batch_epsilon)
        normal = (conv_ref[...] - pooled_ref[0]) * inverse
        normal_ref[...] = normal
        scale_ref[...] = jnp.broadcast_to(vector(0) * inverse, scale_ref.shape)
        region_start = jnp.where(hit_rows(1), vector(3), normal * vector(0) + vector(1))
        start_ref[...] += region_start
        lefts_ref[2] = region_start.astype(jnp.bfloat16)

    @pl.when(step > KINDS)
    def _():
        attend_pair(step - 1 - KINDS, proj_ref, linear_ref, planar_ref, box_ref, merged_ref, probs_ref)

    def along(k):
        return lambda: spread(line, 3, k, 1, stages.along)

    def around(k):
        return lambda: spread(line, 4, k, 0, stages.around)

    def home(k):
        return lambda: spread(line, 4, k, 0, stages.home)

    at_steps(
        [
            (3, [along(0), around(0)]),
            (10, [along(1)]),
            (11, [around(1)]),
            (13, [along(2), home(0)]),
            (15, [around(2), home(1)]),
            (16, [around(3), home(2), home(3), sums.end, stages.end]),
        ]
    )


def forward_layer(
    features, backbone, table, text, hits, vectors, weights, linear_ext, planar_rows, anchor_rows, anchor_cols,
    shards, token_total, collective_id,
):
    dp = lax.axis_size("dp")
    line = dp // RING
    count = len(shards)
    anywhere = pl.BlockSpec(memory_space=pl.ANY)
    width = weights.shape[1]
    page = (PAGE_TOKENS, MODEL_WIDTH)
    f32, bf16 = jnp.float32, jnp.bfloat16

    def pair_at(i):
        return jnp.maximum(i - 1 - KINDS, 0)

    def whole(shape):
        return pl.BlockSpec(shape, lambda i: (0,) * len(shape))

    outs = [
        ((PAGE_TOKENS, width), bf16, whole((PAGE_TOKENS, width))),
        (page, bf16, pl.BlockSpec((PAGE_TOKENS, LANES), lambda i: (0, pair_at(i)))),
        (
            (2, HEADS, PAGE_TOKENS, PAGE_TOKENS), f32,
            pl.BlockSpec((2, 2, PAGE_TOKENS, PAGE_TOKENS), lambda i: (0, pair_at(i), 0, 0)),
        ),
        ((4, *page), bf16, whole((4, *page))),
        (page, f32, whole(page)),
        (page, f32, whole(page)),
        ((8, MODEL_WIDTH), f32, whole((8, MODEL_WIDTH))),
        *(((2 * dp, *shard.shape), shard.dtype, anywhere) for shard in shards),
    ]
    pool = (2, 1, MODEL_WIDTH)
    return pl.pallas_call(
        partial(forward_kernel, line, count, float(token_total)),
        grid=(1 + KINDS + PAIRS,),
        in_specs=[
            once(features.shape),
            once(backbone.shape),
            once(table.shape),
            once(text.shape),
            once(hits.shape),
            once(vectors.shape),
            pl.BlockSpec((MODEL_WIDTH, MODEL_WIDTH), lambda i: (0, column_at_step(i))),
            once(linear_ext.shape),
            once(planar_rows.shape),
            once(anchor_rows.shape),
            once(anchor_cols.shape),
            *[anywhere] * count,
        ],
        out_specs=[spec for shape, kind, spec in outs],
        out_shape=[jax.ShapeDtypeStruct(shape, kind) for shape, kind, spec in outs],
        scratch_shapes=[
            pltpu.VMEM((2, PAGE_TOKENS, PAGE_TOKENS), jnp.int32),
            pltpu.VMEM(page, f32),
            pltpu.VMEM(pool, f32),
            pltpu.VMEM(pool, f32),
            *exchange_scratch(line, pool),
            *gather_sems(line, count),
        ],
        compiler_params=pltpu.CompilerParams(
            collective_id=collective_id, has_side_effects=True, vmem_limit_bytes=62 << 20
        ),
        name="forward_layer",
    )(
        features, backbone, table, text, hits, vectors, weights, linear_ext, planar_rows, anchor_rows, anchor_cols,
        *shards,
    )


TABLE_STEP = PAIRS + KINDS


def backward_kernel(line, count, *refs):
    (
        proj_ref, probs_ref, upstream_ref, rows_ref, cols_ref, lefts_ref, weight_ref, mixer_grad_ref, normal_ref,
        hits_ref,
    ) = refs[:10]
    ins = refs[10 : 10 + count]
    (
        linear_ref, planar_ref, weight_grad_ref, table_grad_ref, text_grad_ref, region_grad_ref, sums_ref,
    ) = refs[10 + count : 17 + count]
    outs = refs[17 + count : 17 + 2 * count]
    grad_ref, turned_left_ref, input_grad_ref = refs[17 + 2 * count : 20 + 2 * count]
    helpers = refs[20 + 2 * count : 24 + 2 * count]
    stages = scatter_stages(line, ins, outs, refs[24 + 2 * count :])
    step = pl.program_id(0)

    @pl.when(step == 0)
    def _():
        greet(line)
        stages.start()
        make_places(rows_ref, cols_ref, *helpers)

    def first(k):
        return lambda: spread(line, 4, k, 0, stages.first)

    def second(k):
        return lambda: spread(line, 4, k, 0, stages.second)

    def third(k):
        return lambda: spread(line, 4, k, 0, stages.third)

    slots = {
        1: [first(0)],
        3: [first(1)],
        7: [second(0)],
        8: [first(2)],
        10: [first(3)],
        12: [second(1)],
        17: [third(0)],
        22: [second(2), second(3)],
    }

    def pump(sub):
        at_steps([(slot // 4, work) for slot, work in slots.items() if slot % 4 == sub])

    @pl.when(step < PAIRS)
    def _():
        attend_back_pair(step, pump, proj_ref, probs_ref, upstream_ref, grad_ref, linear_ref, planar_ref, *helpers)

    @pl.when(jnp.logical_and(step >= PAIRS, step < TABLE_STEP))
    def _():
        column = step - PAIRS
        source = source_of(column)
        fresh = jnp.logical_or(column == 0, source != source_of(jnp.maximum(column - 1, 0)))
        grads = grad_ref[:, pl.ds(pl.multiple_of(column * MODEL_WIDTH, MODEL_WIDTH), MODEL_WIDTH)]

        @pl.when(fresh)
        def _():
            turned_left_ref[...] = lefts_ref[source].T

        weight_grad_ref[...] = dot_nn(turned_left_ref[...], grads).astype(jnp.bfloat16)
        back = dot_nt(grads, weight_ref[...])

        @pl.when(fresh)
        def _():
            input_grad_ref[source] = back

        @pl.when(jnp.logical_not(fresh))
        def _():
            input_grad_ref[source] += back

    @pl.when(step >= TABLE_STEP)
    def _():
        axis = step - TABLE_STEP
        coords = lax.broadcasted_iota(jnp.int32, (COORDS, PAGE_TOKENS), 0)
        total = None
        for stream in range(2):
            hit = (coords == rows_ref[pl.ds(2 * stream + axis, 1), :]).astype(jnp.bfloat16)
            part = dot_nn(hit, input_grad_ref[2 * stream + 1].astype(jnp.bfloat16))
            total = part if total is None else total + part
        table_grad_ref[...] = total.astype(jnp.bfloat16)

    @pl.when(step == TABLE_STEP + 1)
    def _():
        mixer_grad = mixer_grad_ref[...]
        sums_ref[...] = jnp.zeros_like(sums_ref)
        for stream, out_ref in enumerate((text_grad_ref, region_grad_ref)):
            grad = mixer_grad + input_grad_ref[2 * stream]
            hit = jnp.broadcast_to(hits_ref[:, stream : stream + 1] == 1, grad.shape)
            zero = jnp.zeros_like(grad)
            kept = jnp.where(hit, zero, grad)
            out_ref[...] = kept
            sums_ref[stream : stream + 1, :] = jnp.sum(jnp.where(hit, grad, zero), axis=0, keepdims=True)
            if stream == 1:
                sums_ref[2:3, :] = jnp.sum(kept, axis=0, keepdims=True)
                sums_ref[3:4, :] = jnp.sum(kept * normal_ref[...], axis=0, keepdims=True)

    at_steps(
        [(PAIRS + 3, [third(1)]), (PAIRS + 8, [third(2)]), (TABLE_STEP + 1, [third(3), stages.end])]
    )


def backward_layer(
    proj, probs, upstream, anchor_rows, anchor_cols, lefts, weights, mixer_grad, normal, hits, grads, collective_id
):
    dp = lax.axis_size("dp")
    line = dp // RING
    count = len(grads)
    blocks = [(grad.shape[1:], grad.dtype) for grad in grads]
    anywhere = pl.BlockSpec(memory_space=pl.ANY)
    page = (PAGE_TOKENS, MODEL_WIDTH)

    def pair_at(i):
        return jnp.minimum(i, PAIRS - 1)

    def column_at(i):
        return jnp.clip(i - PAIRS, 0, KINDS - 1)

    return pl.pallas_call(
        partial(backward_kernel, line, count),
        grid=(TABLE_STEP + 2,),
        in_specs=[
            once(proj.shape),
            pl.BlockSpec((2, 2, PAGE_TOKENS, PAGE_TOKENS), lambda i: (0, pair_at(i), 0, 0)),
            pl.BlockSpec((PAGE_TOKENS, LANES), lambda i: (0, pair_at(i))),
            once(anchor_rows.shape),
            once(anchor_cols.shape),
            once(lefts.shape),
            pl.BlockSpec((MODEL_WIDTH, MODEL_WIDTH), lambda i: (0, column_at(i))),
            once(page),
            once(page),
            once(hits.shape),
            *[anywhere] * count,
        ],
        out_specs=[
            pl.BlockSpec((HEADS, 1, 2 * PAGE_TOKENS), lambda i: (0, 0, 0)),
            pl.BlockSpec((HEADS, 1, SP_B), lambda i: (0, 0, 0)),
            pl.BlockSpec((MODEL_WIDTH, MODEL_WIDTH), lambda i: (0, column_at(i))),
            pl.BlockSpec((COORDS, MODEL_WIDTH), lambda i: (0, jnp.maximum(i - TABLE_STEP, 0))),
            pl.BlockSpec(page, lambda i: (0, 0)),
            pl.BlockSpec(page, lambda i: (0, 0)),
            pl.BlockSpec((8, MODEL_WIDTH), lambda i: (0, 0)),
            *(pl.BlockSpec(shape, lambda i: (0, 0)) for shape, kind in blocks),
        ],
        out_shape=[
            jax.ShapeDtypeStruct((HEADS, 1, 2 * PAGE_TOKENS), jnp.float32),
            jax.ShapeDtypeStruct((HEADS, 1, SP_B), jnp.float32),
            jax.ShapeDtypeStruct(weights.shape, jnp.bfloat16),
            jax.ShapeDtypeStruct((COORDS, 2 * MODEL_WIDTH), jnp.bfloat16),
            jax.ShapeDtypeStruct(page, jnp.float32),
            jax.ShapeDtypeStruct(page, jnp.float32),
            jax.ShapeDtypeStruct((8, MODEL_WIDTH), jnp.float32),
            *(jax.ShapeDtypeStruct(shape, jnp.float32) for shape, kind in blocks),
        ],
        scratch_shapes=[
            pltpu.VMEM(proj.shape, jnp.bfloat16),
            pltpu.VMEM((MODEL_WIDTH, PAGE_TOKENS), jnp.bfloat16),
            pltpu.VMEM((4, *page), jnp.float32),
            pltpu.VMEM((2, 4 * PAGE_TOKENS, SP_B), jnp.bfloat16),
            pltpu.VMEM((2, 128, PAGE_TOKENS), jnp.bfloat16),
            pltpu.VMEM((2, 4, PAGE_TOKENS, PAGE_TOKENS), jnp.bfloat16),
            pltpu.VMEM((PAGE_TOKENS, PAGE_TOKENS), jnp.bfloat16),
            *scatter_scratch(line, blocks),
        ],
        compiler_params=pltpu.CompilerParams(
            collective_id=collective_id, has_side_effects=True, vmem_limit_bytes=63 << 20
        ),
        name="backward_layer",
    )(
        proj, probs, upstream, anchor_rows, anchor_cols, lefts, weights, mixer_grad, normal, hits,
        *(grad.reshape(line * RING, 2, *grad.shape[1:]) for grad in grads),
    )


def last_kernel(line, count, token_total, *refs):
    sums_ref, kept_ref, normal_ref, scale_ref, features_ref, backbone_ref = refs[:6]
    ins = refs[6 : 6 + count]
    feature_grad_ref, total_ref = refs[6 + count : 8 + count]
    outs = refs[8 + count : 9 + 2 * count]
    turned_ref, conv_grad_ref, late_ref = refs[9 + 2 * count : 12 + 2 * count]
    rest = refs[12 + 2 * count :]
    sums = exchange_stages(line, add_up, sums_ref, total_ref, rest[:7])
    early_scratch = 5 * count + 9
    early = scatter_stages(line, ins, outs[:count], rest[7 : 7 + early_scratch])
    late = scatter_stages(line, [late_ref], outs[count:], rest[7 + early_scratch :])
    share = late_ref.shape[2]

    def first(stages, k):
        spread(line, 4, k, 0, stages.first)

    def second(stages, k):
        spread(line, 4, k, 0, stages.second)

    def third(stages, k):
        spread(line, 4, k, 0, stages.third)

    greet_peers(line)
    sums.near()
    early.start()
    first(early, 0)
    sums.far()
    first(early, 1)
    sums.total()
    conv_grad_ref[...] = (
        scale_ref[...]
        * (kept_ref[...] - total_ref[0:1, :] / token_total - normal_ref[...] * (total_ref[1:2, :] / token_total))
    ).astype(jnp.bfloat16)
    second(early, 0)
    first(early, 2)
    first(early, 3)

    def turn(k, unused):
        columns = pl.ds(pl.multiple_of(k * 512, 512), 512)
        turned_ref[columns, :] = features_ref[:, columns].T
        return unused

    lax.fori_loop(0, features_ref.shape[1] // 512, turn, 0)
    width = min(512, 2 * share * line * RING)

    def backbone(k, unused):
        rows = pl.ds(pl.multiple_of(k * width, width), width)
        block = dot_nn(turned_ref[rows, :], conv_grad_ref[...])
        places = width // (2 * share)
        late_ref[pl.ds(k * places, places)] = block.reshape(places, 2, share, MODEL_WIDTH).astype(jnp.bfloat16)
        return unused

    lax.fori_loop(0, features_ref.shape[1] // width, backbone, 0)
    late.start()
    for k in range(4):
        first(late, k)
    second(early, 1)
    third(early, 0)

    def feature(k, unused):
        columns = pl.ds(pl.multiple_of(k * 512, 512), 512)
        feature_grad_ref[:, columns] = dot_nt(conv_grad_ref[...], backbone_ref[columns, :])
        return unused

    lax.fori_loop(0, features_ref.shape[1] // 512, feature, 0)
    second(early, 2)
    for k in range(4):
        second(late, k)
    second(early, 3)
    third(early, 1)
    third(early, 2)
    for k in range(3):
        third(late, k)
    third(early, 3)
    third(late, 3)
    sums.end()
    early.end()
    late.end()


def last_layer(sums, kept, normal, scale, features, backbone, grads, token_total, collective_id):
    dp = lax.axis_size("dp")
    line = dp // RING
    count = len(grads)
    blocks = [(grad.shape[1:], grad.dtype) for grad in grads]
    channels = backbone.shape[0]
    late = [((channels // (2 * dp), MODEL_WIDTH), jnp.bfloat16)]
    anywhere = pl.BlockSpec(memory_space=pl.ANY)
    vmem = pl.BlockSpec(memory_space=pltpu.VMEM)
    return pl.pallas_call(
        partial(last_kernel, line, count, float(token_total)),
        in_specs=[*[vmem] * 6, *[anywhere] * count],
        out_specs=[vmem] * (3 + count),
        out_shape=[
            jax.ShapeDtypeStruct(features.shape, jnp.float32),
            jax.ShapeDtypeStruct(sums.shape, jnp.float32),
            *(jax.ShapeDtypeStruct(shape, jnp.float32) for shape, kind in blocks + late),
        ],
        scratch_shapes=[
            pltpu.VMEM((channels, PAGE_TOKENS), jnp.bfloat16),
            pltpu.VMEM(kept.shape, jnp.bfloat16),
            pltpu.VMEM((dp, 2, *late[0][0]), jnp.bfloat16),
            *exchange_scratch(line, sums.shape),
            *scatter_scratch(line, blocks),
            *scatter_scratch(line, late),
        ],
        compiler_params=pltpu.CompilerParams(
            collective_id=collective_id, has_side_effects=True, vmem_limit_bytes=63 << 20
        ),
        name="last_layer",
    )(
        sums, kept, normal, scale, features, backbone,
        *(grad.reshape(line * RING, 2, *grad.shape[1:]) for grad in grads),
    )


norm_epsilon = 1e-05


def normal_parts(values):
    center = values - jnp.mean(values, axis=-1, keepdims=True)
    inverse = lax.rsqrt(jnp.mean(center * center, axis=-1, keepdims=True) + norm_epsilon)
    return center * inverse, inverse


def normal_back(normal, inverse, gain, grad):
    scaled = grad * gain
    return inverse * (
        scaled
        - jnp.mean(scaled, axis=-1, keepdims=True)
        - normal * jnp.mean(scaled * normal, axis=-1, keepdims=True)
    )


CHUNKS = 4


def mixer_kernel(
    merged_ref, start_ref, cotangent_ref, vectors_ref, bias_ref, merge_ref, expand_ref, reduce_ref,
    output_ref, mixer_grad_ref, merged_grad_ref, merge_grad_ref, expand_grad_ref, reduce_grad_ref, sums_ref,
    bias_grad_ref,
    hidden_ref, normal_ref, inverse_ref, low_ref, active_ref, slope_ref, dense_ref, grad_ref, grad_low_ref,
    turned_ref,
):
    step = pl.program_id(0)
    chunk = lax.rem(step, CHUNKS)
    width = expand_ref.shape[1] // CHUNKS
    part = pl.ds(pl.multiple_of(chunk * width, width), width)

    def vector(k):
        return vectors_ref[k : k + 1, :]

    def column_sum(values):
        return jnp.sum(values, axis=0, keepdims=True)

    @pl.when(step == 0)
    def _():
        normal, inverse = normal_parts(start_ref[...] + dot_nn(merged_ref[...], merge_ref[...]))
        normal_ref[...] = normal
        inverse_ref[...] = jnp.broadcast_to(inverse, inverse_ref.shape)
        hidden = normal * vector(4) + vector(5)
        hidden_ref[...] = hidden
        low_ref[...] = hidden.astype(jnp.bfloat16)
        dense_ref[...] = jnp.zeros_like(dense_ref)

    @pl.when(step < CHUNKS)
    def _():
        inner = dot_nn(low_ref[...], expand_ref[:, part]) + bias_ref[chunk]
        share = 0.5 + 0.5 * lax.erf(inner * (0.5**0.5))
        active = (inner * share).astype(jnp.bfloat16)
        active_ref[chunk] = active
        slope_ref[chunk] = share + inner * jnp.exp(-0.5 * inner * inner) * (2.0 * jnp.pi) ** -0.5
        dense_ref[...] += dot_nn(active, reduce_ref[part, :])

    @pl.when(step == CHUNKS - 1)
    def _():
        normal, inverse = normal_parts(hidden_ref[...] + (dense_ref[...] + vector(6)))
        output_ref[...] = (normal * vector(7) + vector(8)).astype(jnp.bfloat16)
        upstream = cotangent_ref[...].astype(jnp.float32)
        grad = normal_back(normal, inverse, vector(7), upstream)
        grad_ref[...] = grad
        grad_low_ref[...] = grad.astype(jnp.bfloat16)
        sums_ref[2:3, :] = column_sum(grad)
        sums_ref[3:4, :] = column_sum(upstream * normal)
        sums_ref[4:5, :] = column_sum(upstream)
        turned_ref[...] = low_ref[...].T

    @pl.when(step >= CHUNKS)
    def _():
        grad_low = grad_low_ref[...]
        reduce_grad_ref[...] = dot_tn(active_ref[chunk], grad_low).astype(jnp.bfloat16)
        inner_low = (dot_nt(grad_low, reduce_ref[part, :]) * slope_ref[chunk]).astype(jnp.bfloat16)
        bias_grad_ref[chunk] = column_sum(inner_low.astype(jnp.float32))
        expand_grad_ref[...] = dot_nn(turned_ref[...], inner_low).astype(jnp.bfloat16)
        grad_ref[...] += dot_nt(inner_low, expand_ref[:, part])

    @pl.when(step == 2 * CHUNKS - 1)
    def _():
        grad = grad_ref[...]
        normal = normal_ref[...]
        mixer_grad = normal_back(normal, inverse_ref[:, :1], vector(4), grad)
        mixer_grad_ref[...] = mixer_grad
        sums_ref[0:1, :] = column_sum(grad * normal)
        sums_ref[1:2, :] = column_sum(grad)
        low = mixer_grad.astype(jnp.bfloat16)
        merge_grad_ref[...] = dot_tn(merged_ref[...], low).astype(jnp.bfloat16)
        merged_grad_ref[...] = dot_nt(low, merge_ref[...]).astype(jnp.bfloat16)


def mixer_layer(merged, start, cotangent, vectors, bias, w_merge, w_expand, w_reduce):
    rows = merged.shape[0]
    inner = w_expand.shape[1]
    width = inner // CHUNKS
    page = (rows, MODEL_WIDTH)

    def back_at(i):
        return jnp.maximum(i - CHUNKS, 0)

    def whole(shape):
        return pl.BlockSpec(shape, lambda i: (0,) * len(shape))

    f32, bf16 = jnp.float32, jnp.bfloat16
    outs = [
        (page, bf16, whole(page)),
        (page, f32, whole(page)),
        (page, bf16, whole(page)),
        ((MODEL_WIDTH, MODEL_WIDTH), bf16, whole((MODEL_WIDTH, MODEL_WIDTH))),
        ((MODEL_WIDTH, inner), bf16, pl.BlockSpec((MODEL_WIDTH, width), lambda i: (0, back_at(i)))),
        ((inner, MODEL_WIDTH), bf16, pl.BlockSpec((width, MODEL_WIDTH), lambda i: (back_at(i), 0))),
        ((8, MODEL_WIDTH), f32, whole((8, MODEL_WIDTH))),
        ((CHUNKS, 1, width), f32, whole((CHUNKS, 1, width))),
    ]
    return pl.pallas_call(
        mixer_kernel,
        grid=(2 * CHUNKS,),
        in_specs=[
            once(page),
            once(page),
            once(page),
            once(vectors.shape),
            once(bias.shape),
            once(w_merge.shape),
            once(w_expand.shape),
            once(w_reduce.shape),
        ],
        out_specs=[spec for shape, kind, spec in outs],
        out_shape=[jax.ShapeDtypeStruct(shape, kind) for shape, kind, spec in outs],
        scratch_shapes=[
            pltpu.VMEM(page, f32),
            pltpu.VMEM(page, f32),
            pltpu.VMEM((rows, 128), f32),
            pltpu.VMEM(page, bf16),
            pltpu.VMEM((CHUNKS, rows, width), bf16),
            pltpu.VMEM((CHUNKS, rows, width), f32),
            pltpu.VMEM(page, f32),
            pltpu.VMEM(page, f32),
            pltpu.VMEM(page, bf16),
            pltpu.VMEM((MODEL_WIDTH, rows), bf16),
        ],
        compiler_params=pltpu.CompilerParams(vmem_limit_bytes=62 << 20),
        name="mixer_layer",
    )(merged, start, cotangent, vectors, bias, w_merge, w_expand, w_reduce)

AXES = ("dp", "pair")


def padded_rows(pieces):
    rows = [jnp.pad(piece.astype(jnp.float32), ((0, 0), (0, 128 - piece.shape[1]))) for piece in pieces]
    total = sum(piece.shape[0] for piece in pieces)
    rows.append(jnp.zeros((-total % 8, 128), jnp.float32))
    return jnp.concatenate(rows, axis=0)


def blocks_of(grad, devices):
    blocks = grad.astype(jnp.bfloat16).reshape(devices, grad.shape[0] // devices, grad.shape[1])
    return blocks if blocks.shape[1] % 8 == 0 else blocks.reshape(devices, -1, 128)


def per_device(
    text_inputs,
    region_features,
    text_masked,
    region_masked,
    text_anchors,
    region_anchors,
    backbone_weight,
    batch_gain,
    batch_shift,
    text_blank,
    region_blank,
    position_table,
    stream_weights,
    linear_bias,
    planar_bias,
    merge_weight,
    mixer_gain,
    mixer_shift,
    expand_weight,
    expand_bias,
    reduce_weight,
    reduce_bias,
    output_gain,
    output_shift,
    cotangent,
):
    devices = lax.axis_size(AXES)
    row_count = text_inputs.shape[0]
    token_total = row_count * devices
    share = MODEL_WIDTH // devices
    expand_share = expand_bias.shape[0]
    bias_rows = REL_B // devices
    vectors = jnp.stack(
        [
            batch_gain, batch_shift, text_blank, region_blank, mixer_gain, mixer_shift, reduce_bias,
            output_gain, output_shift,
        ]
    )
    small = padded_rows([linear_bias, planar_bias, vectors, expand_bias[None, :]])
    packed, w_backbone, w_table, w_stream = gather_all(
        (small, backbone_weight, position_table, stream_weights), 0
    )
    w_linear = packed[:, :bias_rows, :HEADS].reshape(REL_B, HEADS)
    w_planar = packed[:, bias_rows : 2 * bias_rows, :HEADS].reshape(SP_B, HEADS)
    w_vectors = packed[:, 2 * bias_rows : 2 * bias_rows + 9, :share].transpose(1, 0, 2).reshape(9, -1)
    w_expand_bias = packed[:, 2 * bias_rows + 9, :expand_share].reshape(-1)
    w_backbone, w_table, w_stream = (
        whole.reshape(-1, whole.shape[-1]) for whole in (w_backbone, w_table, w_stream)
    )

    anchor_rows = jnp.concatenate([text_anchors, region_anchors], axis=0)
    anchor_cols = anchor_rows.T
    hits = jnp.stack([text_masked, region_masked], axis=1)
    proj, merged_low, probs, lefts, start_sum, normal_feat, batch_scale, *wholes = forward_layer(
        region_features, w_backbone, w_table, text_inputs, hits, w_vectors, w_stream, linear_extended(w_linear),
        w_planar.T[:, None, :], anchor_rows, anchor_cols, (merge_weight, expand_weight, reduce_weight),
        token_total, 4,
    )
    w_merge, w_expand, w_reduce = (whole.reshape(-1, whole.shape[-1]) for whole in wholes)
    (
        layer_output, mixer_in_grad, merged_grad, merge_weight_grad, expand_weight_grad, reduce_weight_grad,
        mixer_sums, expand_bias_grad,
    ) = mixer_layer(
        merged_low, start_sum, cotangent, w_vectors, w_expand_bias.reshape(CHUNKS, 1, -1),
        w_merge, w_expand, w_reduce,
    )
    early = (expand_weight_grad, reduce_weight_grad, merge_weight_grad)
    (
        linear_sums, planar_sums, stream_weights_grad, position_table_grad, text_gradient, region_kept,
        start_sums, *early_shares,
    ) = backward_layer(
        proj, probs, merged_grad, anchor_rows, anchor_cols, lefts, w_stream, mixer_in_grad, normal_feat, hits,
        [blocks_of(grad, devices) for grad in early], 5,
    )
    expand_weight_grad, reduce_weight_grad, merge_weight_grad = (
        part.reshape(-1, grad.shape[1]) for part, grad in zip(early_shares, early)
    )
    vector_grads = jnp.concatenate([start_sums[:2], mixer_sums[:5]], axis=0)
    pieces = [
        linear_folded(linear_sums[:, 0]).T.reshape(devices, bias_rows, HEADS),
        planar_sums[:, 0].T.reshape(devices, bias_rows, HEADS),
        vector_grads.reshape(7, devices, share).transpose(1, 0, 2),
        expand_bias_grad.reshape(devices, 1, expand_share),
    ]
    small_grads = jax.vmap(lambda *parts: padded_rows(parts))(*pieces)
    late = (stream_weights_grad, position_table_grad)
    feature_gradient, totals, small, *shares = last_layer(
        start_sums[2:4], region_kept, normal_feat, batch_scale[:1], region_features,
        w_backbone, [small_grads, *(blocks_of(grad, devices) for grad in late)], token_total, 1,
    )
    stream_weights_grad, position_table_grad = (
        part.reshape(-1, grad.shape[1]) for part, grad in zip(shares, late)
    )
    backbone_weight_grad = shares[2]
    owned = lax.dynamic_slice_in_dim(totals, lax.axis_index(AXES) * share, share, axis=1)
    batch_shift_gradient = owned[0]
    batch_gain_gradient = owned[1]
    vector_shares = small[2 * bias_rows : 2 * bias_rows + 7, :share]
    return (
        layer_output,
        text_gradient,
        feature_gradient,
        backbone_weight_grad,
        batch_gain_gradient,
        batch_shift_gradient,
        vector_shares[0],
        vector_shares[1],
        position_table_grad,
        stream_weights_grad,
        small[:bias_rows, :HEADS],
        small[bias_rows : 2 * bias_rows, :HEADS],
        merge_weight_grad,
        vector_shares[2],
        vector_shares[3],
        expand_weight_grad,
        small[2 * bias_rows + 7, :expand_share],
        reduce_weight_grad,
        vector_shares[4],
        vector_shares[5],
        vector_shares[6],
    )


def solution(mesh):
    in_specs = (
        P(("dp", "pair"), None),
        P(("dp", "pair"), None),
        P(("dp", "pair")),
        P(("dp", "pair")),
        P(None, ("dp", "pair")),
        P(None, ("dp", "pair")),
        P(("dp", "pair"), None),
        P(("dp", "pair")),
        P(("dp", "pair")),
        P(("dp", "pair")),
        P(("dp", "pair")),
        P(("dp", "pair"), None),
        P(("dp", "pair"), None),
        P(("dp", "pair"), None),
        P(("dp", "pair"), None),
        P(("dp", "pair"), None),
        P(("dp", "pair")),
        P(("dp", "pair")),
        P(("dp", "pair"), None),
        P(("dp", "pair")),
        P(("dp", "pair"), None),
        P(("dp", "pair")),
        P(("dp", "pair")),
        P(("dp", "pair")),
        P(("dp", "pair"), None),
    )
    out_specs = (
        P(("dp", "pair"), None),
        P(("dp", "pair"), None),
        P(("dp", "pair"), None),
        P(("dp", "pair"), None),
        P(("dp", "pair")),
        P(("dp", "pair")),
        P(("dp", "pair")),
        P(("dp", "pair")),
        P(("dp", "pair"), None),
        P(("dp", "pair"), None),
        P(("dp", "pair"), None),
        P(("dp", "pair"), None),
        P(("dp", "pair"), None),
        P(("dp", "pair")),
        P(("dp", "pair")),
        P(("dp", "pair"), None),
        P(("dp", "pair")),
        P(("dp", "pair"), None),
        P(("dp", "pair")),
        P(("dp", "pair")),
        P(("dp", "pair")),
    )
    return jax.shard_map(
        per_device, mesh=mesh, in_specs=in_specs, out_specs=out_specs, check_vma=False
    )
```

profile of v0, /device:TPU:8, one launch (start us, length us, event | category | flops | bytes accessed | tf_op | source)
XLA Modules:
  0.0 353.7 jit_solution(3037447344222551083)
XLA Ops:
  0.7 0.7 pad_convert_fusion.3
  1.3 0.7 pad_add_fusion.1
  2.0 0.7 pad_add_fusion.refs_9_.refs_3_
  2.7 1.5 stack.48
  4.2 0.7 pad_convert_fusion.1
  4.9 3.1 concatenate.18.refs_0_
  8.0 0.8 copy.77.refs_4_.refs_9_
  8.8 0.8 copy.76
  9.6 84.0 %gather_all.1 = (f32[32,32,128]{2,1,0:T(8,128)}, bf16[32,64,768]{2,1,0:T(8,128)(2,1)}, bf16[32,32,1536]{2,1,0:T(8,128)(2,1)}, bf16[32,24,7680]{2,1,0:T(8,128)(2,1)}) custom-call(f32[32,128]{1,0:T(8,128)} %concatenate.18.refs_0_, bf16[64,768]{1,0:T(8,128)(2,1)} %refs_1_.1, bf16[32,1536]{1,0:T(8,128)(2,1)} %refs_2_.1, bf16[24,7680]{1,0:T(8,128)(2,1)} %refs_3_.2), custom_call_target="tpu_custom_call" | custom-call | tf_op jit(solution)/shard_map/gather_all/pallas_call | solution.py:428
  93.6 1.0 slice_reduce_fusion.1
  94.6 0.7 reshape_reshape_squeeze.3.bias_ref
  95.2 1.0 slice_bitcast_fusion
  96.2 1.0 slice_bitcast_fusion.1
  97.3 0.7 reshape.88.refs_5_.vectors_ref
  98.1 0.6 broadcast_in_dim.36.refs_8_
  98.8 0.2 slice_reduce_fusion.4
  99.1 0.1 pad_maximum_fusion
  99.2 0.6 broadcast_in_dim.35.refs_7_
  99.8 60.0 %forward_layer.1 = (bf16[256,7680]{1,0:T(8,128)(2,1)}, bf16[256,768]{1,0:T(8,128)(2,1)}, f32[2,12,256,256]{3,2,1,0:T(8,128)}, bf16[4,256,768]{2,1,0:T(8,128)(2,1...) custom-call(bf16[256,2048]{1,0:T(8,128)(2,1)} %refs_4_.1, ...), custom_call_target="tpu_custom_call" | custom-call | tf_op jit(solution)/shard_map/forward_layer/pallas_call | solution.py:921
  159.8 1.3 slice.90.refs_3_
  161.2 20.7 %mixer_layer.1 = (bf16[256,768]{1,0:T(8,128)(2,1)}, f32[256,768]{1,0:T(8,128)}, bf16[256,768]{1,0:T(8,128)(2,1)}, bf16[768,768]{1,0:T(8,128)(2,1)}, bf16[768,307...) custom-call(bf16[256,768]{1,0:T(8,128)(2,1)} %get-tuple-element.63.merged_ref, ...), custom_call_target="tpu_custom_call" | custom-call | tf_op jit(solution)/shard_map/mixer_layer/pallas_call | solution.py:1366
  181.9 62.8 %backward_layer.1 = (f32[12,1,512]{2,1,0:T(1,128)}, f32[12,1,256]{2,1,0:T(1,128)}, bf16[768,7680]{1,0:T(8,128)(2,1)}, bf16[1024,1536]{1,0:T(8,128)(2,1)}, f32[25...) custom-call(bf16[256,7680]{1,0:T(8,128)(2,1)} %get-tuple-element.69., ...), custom_call_target="tpu_custom_call" | custom-call | tf_op jit(solution)/shard_map/backward_layer/pallas_call | solution.py:1078
  244.8 0.1 reshape.98
  244.8 1.4 fusion.2
  246.3 0.7 copy.96
  247.0 0.2 slice_reduce_fusion
  247.2 0.1 slice_reduce_fusion.2
  247.3 0.1 copy.79
  247.4 0.1 copy.80
  247.5 0.1 maximum_bitcast_fusion
  247.6 0.1 reshape.97
  247.8 0.1 copy.92
  247.9 0.8 copy.94
  248.7 0.8 select_maximum_fusion
  249.5 90.5 %last_layer.1 = (f32[256,2048]{1,0:T(8,128)}, f32[2,768]{1,0:T(2,128)}, f32[24,128]{1,0:T(8,128)}, f32[24,7680]{1,0:T(8,128)}, f32[32,1536]{1,0:T(8,128)}, /*index=5*/f32[64,768]{1,0:T(8,128)}) custom-call(f32[2,768]{1,0:T(2,128)} %get-tuple-element.102.refs_0_, f32[256,768]{1,0:T(8,128)} %get-tuple-element.80.refs_1_, ...), custom_call_target="tpu_custom_call" | custom-call | tf_op jit(solution)/shard_map/last_layer/pallas_call | solution.py:1223
  340.0 0.9 constant_dynamic-slice_fusion
  340.9 0.5 slice_bitcast_fusion.11
  341.4 1.2 slice_bitcast_fusion.6
  342.6 1.5 slice_bitcast_fusion.3
  344.1 1.3 fusion.3
  345.3 0.9 copy.105
  346.2 3.2 copy.106
  349.4 0.7 copy.107
  350.1 0.7 copy.108
  350.8 0.9 copy.109
  351.6 0.6 copy.110
  352.3 0.7 copy.111
  353.0 0.7 copy.112
  (31 shorter events, 0.5 us)
Async XLA Ops:
  2.7 97.1 %copy-start.7 = (s32[4,256]{1,0:T(4,128)}, s32[4,256]{1,0:T(4,128)S(1)}, u32[]{:S(2)}) copy-start(s32[4,256]{1,0:T(4,128)S(1)} %pad_add_fusion.refs_9_.refs_3_) | copy-start | bytes 12292
  181.9 62.8 %copy-start.9 = (f32[4,1,768]{2,1,0:T(1,128)S(1)}, f32[4,1,768]{2,1,0:T(1,128)}, u32[]{:S(2)}) copy-start(f32[4,1,768]{2,1,0:T(1,128)} %get-tuple-element.85) | copy-start | bytes 36868
  181.9 64.4 %copy-start.8 = (f32[8,768]{1,0:T(8,128)S(1)}, f32[8,768]{1,0:T(8,128)}, u32[]{:S(2)}) copy-start(f32[8,768]{1,0:T(8,128)} %get-tuple-element.84) | copy-start | bytes 73732
  249.5 95.8 %copy-start = (f32[256,768]{1,0:T(8,128)S(1)}, f32[256,768]{1,0:T(8,128)}, u32[]{:S(2)}) copy-start(f32[256,768]{1,0:T(8,128)} %get-tuple-element.138) | copy-start | bytes 2359300
  340.0 9.4 %copy-start.5 = (f32[64,768]{1,0:T(8,128)S(1)}, f32[64,768]{1,0:T(8,128)}, u32[]{:S(2)}) copy-start(f32[64,768]{1,0:T(8,128)} %get-tuple-element.140) | copy-start | bytes 589828
  340.0 10.1 %copy-start.4 = (f32[32,1536]{1,0:T(8,128)S(1)}, f32[32,1536]{1,0:T(8,128)}, u32[]{:S(2)}) copy-start(f32[32,1536]{1,0:T(8,128)} %get-tuple-element.145) | copy-start | bytes 589828
  340.0 10.8 %copy-start.1 = (f32[24,7680]{1,0:T(8,128)S(1)}, f32[24,7680]{1,0:T(8,128)}, u32[]{:S(2)}) copy-start(f32[24,7680]{1,0:T(8,128)} %get-tuple-element.146) | copy-start | bytes 2211844
  345.3 6.3 %copy-start.6 = (f32[24,768]{1,0:T(8,128)S(1)}, f32[24,768]{1,0:T(8,128)}, u32[]{:S(2)}) copy-start(f32[24,768]{1,0:T(8,128)} %get-tuple-element.149) | copy-start | bytes 221188
  345.3 6.9 %copy-start.3 = (f32[24,3072]{1,0:T(8,128)S(1)}, f32[24,3072]{1,0:T(8,128)}, u32[]{:S(2)}) copy-start(f32[24,3072]{1,0:T(8,128)} %get-tuple-element.152) | copy-start | bytes 884740
  346.2 6.8 %copy-start.2 = (f32[96,768]{1,0:T(8,128)S(1)}, f32[96,768]{1,0:T(8,128)}, u32[]{:S(2)}) copy-start(f32[96,768]{1,0:T(8,128)} %get-tuple-element.154) | copy-start | bytes 884740
where the time goes:
time: 358 us; the launch traced here: 354 us
  Pallas kernels  318 us (89%)
  local copies, waits for them, and re-layouts  30.8 us (9%)
  other arithmetic  4.09 us (1%)
    pallas_call x1, Pallas kernels, last_layer(): pl.pallas_call(partial(last_kernel, line, count, float(token_total)), in_...  90.5 us
    pallas_call x1, Pallas kernels, gather_all(): pl.pallas_call(partial(gather_kernel, line, count), in_specs=[pl.BlockSpe...  84 us
    pallas_call x1, Pallas kernels, backward_layer(): pl.pallas_call(partial(backward_kernel, line, count), grid=(TABLE_STEP +...  62.8 us
    pallas_call x1, Pallas kernels, forward_layer(): pl.pallas_call(partial(forward_kernel, line, count, float(token_total)),...  60 us
    pallas_call x1, Pallas kernels, mixer_layer(): pl.pallas_call(mixer_kernel, grid=(2 * CHUNKS,), in_specs=[once(page), on...  20.7 us
    unnamed x31, local copies, waits for them, and re-layouts  9.31 us

commit v1 on v0

--- a/solution.py
+++ b/solution.py
@@ -168,13 +168,6 @@
         )
 
 
-def linear_extended(linear_bias):
-    rows = linear_bias.astype(jnp.float32).T
-    low = jnp.broadcast_to(rows[:, :1], (HEADS, PAGE_TOKENS - 1 - REL_B // 2))
-    high = jnp.broadcast_to(rows[:, -1:], (HEADS, PAGE_TOKENS - REL_B // 2 + 1))
-    return jnp.concatenate([low, rows, high], axis=1)[:, None, :]
-
-
 def linear_folded(sums):
     first = REL_B // 2
     last = PAGE_TOKENS - 1 + REL_B // 2 - 1
@@ -396,12 +389,140 @@
     ]
 
 
-def gather_kernel(line, count, *refs):
-    stages = gather_stages(line, refs[:count], refs[count : 2 * count], refs[2 * count :])
+def group_of(zz):
+    return pl.ds(zz * RING, RING)
+
+
+def flat_gather_stages(line, ins, outs, sems):
+    count = len(ins)
+    own_sem, xy_send, xy_recv, d_send, d_recv, z_send, z_recv, c_send, c_recv = sems
+    z, q, c = place()
+    beside = (across(q, 1), across(q, 2))
+    corner = across(across(q, 1), 2)
+
+    def remote(src, dst, send, recv, zz, qq, cc):
+        return pltpu.make_async_remote_copy(
+            src_ref=src, dst_ref=dst, send_sem=send, recv_sem=recv,
+            device_id={"dp": zz * RING + qq, "pair": cc}, device_id_type=MESH,
+        )
+
+    def block(a, qq):
+        return outs[a].at[z * RING + qq, c]
+
+    def halves(a):
+        width = ins[a].shape[-1]
+        return (0, width // 2), (width // 2, width // 2)
+
+    def own(a):
+        return pltpu.make_async_copy(ins[a], block(a, q), own_sem.at[a])
+
+    def xy_copy(a, axis):
+        return remote(ins[a], block(a, q), xy_send.at[axis, a], xy_recv.at[axis, a], z, beside[axis], c)
+
+    def xy_got(a, axis):
+        got = block(a, beside[axis])
+        return remote(got, got, xy_send.at[axis, a], xy_recv.at[axis, a], z, beside[axis], c)
+
+    def d_copy(a, axis, qq):
+        start, width = halves(a)[axis]
+        part = outs[a].at[z * RING + qq, c, :, pl.ds(start, width)]
+        return remote(part, part, d_send.at[axis, a], d_recv.at[axis, a], z, beside[1 - axis], c)
+
+    def z_copy(a, way, zz, target):
+        part = outs[a].at[group_of(zz), c]
+        return remote(part, part, z_send.at[way, a, zz], z_recv.at[way, a, zz], target, q, c)
+
+    def c_copy(a, zz, cc):
+        part = outs[a].at[group_of(zz), cc]
+        return remote(part, part, c_send.at[a, zz], c_recv.at[a, zz], z, q, 1 - c)
+
+    def ahead(way):
+        return z < line - 1 if way == 0 else z > 0
+
+    def start():
+        for a in range(count):
+            own(a).start()
+            for axis in range(2):
+                xy_copy(a, axis).start()
+
+    def around():
+        for a in range(count):
+            for axis in range(2):
+                xy_got(a, axis).wait_recv()
+                d_copy(a, axis, beside[axis]).start()
+
+    def home():
+        for a in range(count):
+            own(a).wait()
+            for axis in range(2):
+                d_copy(a, axis, corner).wait_recv()
+            for way in range(2):
+                @pl.when(ahead(way))
+                def _():
+                    z_copy(a, way, z, z + 1 - 2 * way).start()
+            c_copy(a, z, c).start()
+
+    def along(g):
+        for a in range(count):
+            for way in range(2):
+                zz = z - g if way == 0 else z + g
+
+                @pl.when(zz >= 0 if way == 0 else zz <= line - 1)
+                def _():
+                    z_copy(a, way, zz, z - 1 + 2 * way).wait_recv()
+
+                    @pl.when(ahead(way))
+                    def _():
+                        z_copy(a, way, zz, z + 1 - 2 * way).start()
+
+                    c_copy(a, zz, c).start()
+
+    def end():
+        for a in range(count):
+            for axis in range(2):
+                xy_copy(a, axis).wait_send()
+                d_copy(a, axis, beside[axis]).wait_send()
+
+            def drain(zz, unused):
+                c_copy(a, zz, c).wait_send()
+                c_copy(a, zz, 1 - c).wait_recv()
+                for way in range(2):
+                    @pl.when(jnp.logical_and(ahead(way), zz <= z if way == 0 else zz >= z))
+                    def _():
+                        z_copy(a, way, zz, z + 1 - 2 * way).wait_send()
+                return unused
+
+            lax.fori_loop(0, line, drain, 0)
+
+    return SimpleNamespace(start=start, around=around, home=home, along=along, end=end)
+
+
+def flat_gather_sems(line, count):
+    dma = pltpu.SemaphoreType.DMA
+    return [
+        dma((count,)),
+        *(dma((2, count)) for k in range(4)),
+        *(dma((2, count, line)) for k in range(2)),
+        *(dma((count, line)) for k in range(2)),
+    ]
+
+
+def gather_kernel(line, count, flat, *refs):
+    both = count + flat
+    ins, outs, sems = refs[:both], refs[both : 2 * both], refs[2 * both :]
+    stages = gather_stages(line, ins[:count], outs[:count], sems[:9])
+    plane = flat_gather_stages(line, ins[count:], outs[count:], sems[9:])
     greet(line)
+    plane.start()
     stages.start()
+    plane.around()
+    plane.home()
 
     def generation(g, unused):
+        @pl.when(jnp.logical_and(g >= 2, g <= line))
+        def _():
+            plane.along(g - 1)
+
         @pl.when(g <= line - 1)
         def _():
             stages.along(g)
@@ -418,22 +539,26 @@
 
     lax.fori_loop(1, line + 2, generation, 0)
     stages.end()
-
-
-def gather_all(shards, collective_id):
+    plane.end()
+
+
+def gather_all(shards, flat_shards, collective_id):
     dp = lax.axis_size("dp")
     line = dp // RING
-    devices = 2 * dp
-    count = len(shards)
-    return pl.pallas_call(
-        partial(gather_kernel, line, count),
-        in_specs=[pl.BlockSpec(memory_space=pl.ANY)] * count,
-        out_specs=[pl.BlockSpec(memory_space=pl.ANY)] * count,
-        out_shape=[jax.ShapeDtypeStruct((devices, *shard.shape), shard.dtype) for shard in shards],
-        scratch_shapes=gather_sems(line, count),
+    count, flat = len(shards), len(flat_shards)
+    wholes = pl.pallas_call(
+        partial(gather_kernel, line, count, flat),
+        in_specs=[pl.BlockSpec(memory_space=pl.ANY)] * (count + flat),
+        out_specs=[pl.BlockSpec(memory_space=pl.ANY)] * (count + flat),
+        out_shape=[
+            *(jax.ShapeDtypeStruct((2 * dp, *shard.shape), shard.dtype) for shard in shards),
+            *(jax.ShapeDtypeStruct((dp, 2, *shard.shape), shard.dtype) for shard in flat_shards),
+        ],
+        scratch_shapes=[*gather_sems(line, count), *flat_gather_sems(line, flat)],
         compiler_params=pltpu.CompilerParams(collective_id=collective_id, has_side_effects=True),
         name="gather_all",
-    )(*shards)
+    )(*shards, *flat_shards)
+    return [whole.reshape(2 * dp, *whole.shape[-2:]) for whole in wholes]
 
 
 def scatter_stages(line, ins, outs, scratch):
@@ -604,46 +729,157 @@
     ]
 
 
-def scatter_kernel(line, count, *refs):
-    stages = scatter_stages(line, refs[:count], refs[count : 2 * count], refs[2 * count :])
-    greet(line)
-    stages.start()
-
-    def generation(step, unused):
-        @pl.when(step < line)
+def flat_scatter_stages(line, ins, outs, scratch):
+    count = len(ins)
+    mine, beside_sum, line_in, half_in, full_in = (scratch[k * count : (k + 1) * count] for k in range(5))
+    own_sem, c_send, c_recv, z_send, z_recv, d_send, d_recv, xy_send, xy_recv = scratch[5 * count :]
+    z, q, c = place()
+    beside = (across(q, 1), across(q, 2))
+    corner = across(across(q, 1), 2)
+
+    def remote(src, dst, send, recv, zz, qq, cc):
+        return pltpu.make_async_remote_copy(
+            src_ref=src, dst_ref=dst, send_sem=send, recv_sem=recv,
+            device_id={"dp": zz * RING + qq, "pair": cc}, device_id_type=MESH,
+        )
+
+    def halves(a):
+        width = outs[a].shape[-1]
+        cut = width // 2 if width % 256 == 0 else width
+        return (0, cut), (cut, width - cut)
+
+    def own(a, zz):
+        return pltpu.make_async_copy(ins[a].at[group_of(zz), c], mine[a].at[group_of(zz)], own_sem.at[a, zz])
+
+    def c_copy(a, zz):
+        return remote(
+            ins[a].at[group_of(zz), 1 - c], beside_sum[a].at[group_of(zz)], c_send.at[a, zz], c_recv.at[a, zz],
+            z, q, 1 - c,
+        )
+
+    def z_copy(a, way, zz):
+        return remote(
+            mine[a].at[group_of(zz)], line_in[a].at[way, group_of(zz)], z_send.at[way, a, zz],
+            z_recv.at[way, a, zz], z + 1 - 2 * way, q, c,
+        )
+
+    def d_copy(a, axis):
+        start, width = halves(a)[axis]
+        return remote(
+            mine[a].at[z * RING + corner, :, pl.ds(start, width)], half_in[a].at[:, pl.ds(start, width)],
+            d_send.at[axis, a], d_recv.at[axis, a], z, beside[axis], c,
+        )
+
+    def xy_copy(a, axis):
+        return remote(
+            mine[a].at[z * RING + beside[axis]], full_in[a].at[axis], xy_send.at[axis, a], xy_recv.at[axis, a],
+            z, beside[axis], c,
+        )
+
+    def behind(way):
+        return z > 0 if way == 0 else z < line - 1
+
+    def both_ways(g, work):
+        @pl.when(z - g >= 0)
         def _():
-            stages.first(step)
-
-        @pl.when(jnp.logical_and(step >= 1, step <= line))
+            work(z - g)
+
+        @pl.when(jnp.logical_and(z + g <= line - 1, g > 0))
         def _():
-            stages.second(step - 1)
-
-        @pl.when(step >= 2)
-        def _():
-            stages.third(step - 2)
-
-        return unused
-
-    lax.fori_loop(0, line + 2, generation, 0)
-    stages.end()
-
-
-def scatter_all(grads, collective_id):
-    dp = lax.axis_size("dp")
-    line = dp // RING
-    count = len(grads)
-    blocks = [(grad.shape[1:], grad.dtype) for grad in grads]
-    return pl.pallas_call(
-        partial(scatter_kernel, line, count),
-        in_specs=[pl.BlockSpec(memory_space=pl.ANY)] * count,
-        out_specs=[pl.BlockSpec(memory_space=pltpu.VMEM)] * count,
-        out_shape=[jax.ShapeDtypeStruct(shape, jnp.float32) for shape, kind in blocks],
-        scratch_shapes=scatter_scratch(line, blocks),
-        compiler_params=pltpu.CompilerParams(
-            collective_id=collective_id, has_side_effects=True, vmem_limit_bytes=63 << 20
-        ),
-        name="scatter_all",
-    )(*(grad.reshape(line * RING, 2, *grad.shape[1:]) for grad in grads))
+            work(z + g)
+
+    def add(a, zz, part):
+        def one(qq, unused):
+            k = zz * RING + qq
+            mine[a][k] = mine[a][k] + part[k]
+            return unused
+
+        lax.fori_loop(0, RING, one, 0)
+
+    def begin(zz):
+        for a in range(count):
+            c_copy(a, zz).start()
+            own(a, zz).start()
+
+    def first(zz):
+        for a in range(count):
+            own(a, zz).wait()
+            c_copy(a, zz).wait_recv()
+            add(a, zz, beside_sum[a])
+            for way in range(2):
+                @pl.when(jnp.logical_and(behind(way), zz >= z if way == 0 else zz <= z))
+                def _():
+                    z_copy(a, way, zz).wait_recv()
+                    add(a, zz, line_in[a].at[way])
+
+                @pl.when(zz > z if way == 0 else zz < z)
+                def _():
+                    z_copy(a, way, zz).start()
+
+            @pl.when(zz == z)
+            def _():
+                for axis in range(2):
+                    if halves(a)[axis][1]:
+                        d_copy(a, axis).start()
+
+    def second():
+        for a in range(count):
+            for axis in range(2):
+                start, width = halves(a)[axis]
+                k = z * RING + beside[1 - axis]
+                if width:
+                    d_copy(a, axis).wait_recv()
+                    mine[a][k, :, start : start + width] = (
+                        mine[a][k, :, start : start + width] + half_in[a][:, start : start + width]
+                    )
+                xy_copy(a, 1 - axis).start()
+
+    def third():
+        for a in range(count):
+            for axis in range(2):
+                xy_copy(a, axis).wait_recv()
+            outs[a][...] = sum(
+                part.astype(jnp.float32) for part in (mine[a][z * RING + q], full_in[a][0], full_in[a][1])
+            )
+
+    def start():
+        lax.fori_loop(0, line, lambda step, unused: (both_ways(line - 1 - step, begin), unused)[1], 0)
+
+    def end():
+        for a in range(count):
+            for axis in range(2):
+                if halves(a)[axis][1]:
+                    d_copy(a, axis).wait_send()
+                xy_copy(a, axis).wait_send()
+
+            def drain(zz, unused):
+                c_copy(a, zz).wait_send()
+                for way in range(2):
+                    @pl.when(zz > z if way == 0 else zz < z)
+                    def _():
+                        z_copy(a, way, zz).wait_send()
+                return unused
+
+            lax.fori_loop(0, line, drain, 0)
+
+    return SimpleNamespace(
+        start=start, first=lambda step: both_ways(line - 1 - step, first), second=second, third=third, end=end
+    )
+
+
+def flat_scatter_scratch(line, blocks):
+    dma = pltpu.SemaphoreType.DMA
+    count = len(blocks)
+    return [
+        *(pltpu.VMEM((line * RING, *shape), kind) for shape, kind in blocks),
+        *(pltpu.VMEM((line * RING, *shape), kind) for shape, kind in blocks),
+        *(pltpu.VMEM((2, line * RING, *shape), kind) for shape, kind in blocks),
+        *(pltpu.VMEM(shape, kind) for shape, kind in blocks),
+        *(pltpu.VMEM((2, *shape), kind) for shape, kind in blocks),
+        *(dma((count, line)) for k in range(3)),
+        *(dma((2, count, line)) for k in range(2)),
+        *(dma((2, count)) for k in range(4)),
+    ]
 
 
 def peers(line):
@@ -797,16 +1033,58 @@
     return jnp.where(turn >= 7, turn - 2, jnp.where(turn >= 5, turn + 3, turn))
 
 
+VECTORS = 9
+CHUNKS = 4
+
+
+def unpack(packed_ref, vectors_ref, bias_ref, linear_ref, planar_ref):
+    devices = packed_ref.shape[0]
+    bias_rows = REL_B // devices
+
+    def row(k):
+        return packed_ref[:, k, :].astype(jnp.bfloat16)
+
+    def lined_up(k, share, first):
+        lane = lax.broadcasted_iota(jnp.int32, (128, MODEL_WIDTH), 1)
+        spread = (lax.broadcasted_iota(jnp.int32, (128, MODEL_WIDTH), 0) == lax.rem(lane, share)).astype(jnp.bfloat16)
+        owner = lax.broadcasted_iota(jnp.int32, (devices, MODEL_WIDTH), 1) // share + first
+        mine = lax.broadcasted_iota(jnp.int32, (devices, MODEL_WIDTH), 0) == owner
+        whole = dot_nn(row(k), spread)
+        return jnp.sum(jnp.where(mine, whole, jnp.zeros_like(whole)), axis=0, keepdims=True)
+
+    def table(first, width, shift):
+        bucket = jnp.clip(lax.broadcasted_iota(jnp.int32, (devices, width), 1) - shift, 0, REL_B - 1)
+        start = lax.broadcasted_iota(jnp.int32, (devices, width), 0) * bias_rows
+        total = None
+        for k in range(bias_rows):
+            part = dot_tn(row(first + k), (bucket == start + k).astype(jnp.bfloat16))
+            total = part if total is None else total + part
+        return total
+
+    vectors_ref[...] = jnp.zeros_like(vectors_ref)
+    for k in range(VECTORS):
+        vectors_ref[k : k + 1, :] = lined_up(2 * bias_rows + k, MODEL_WIDTH // devices, 0)
+    share = CHUNKS * MODEL_WIDTH // devices
+    for k in range(CHUNKS):
+        bias_ref[k] = lined_up(2 * bias_rows + VECTORS, share, k * (MODEL_WIDTH // share))
+    linear = table(0, 2 * PAGE_TOKENS, PAGE_TOKENS - 1 - REL_B // 2)
+    planar = table(bias_rows, SP_B, 0)
+    for head in range(HEADS):
+        linear_ref[head] = linear[head : head + 1, :]
+        planar_ref[head] = planar[head : head + 1, :]
+
+
 def forward_kernel(line, count, token_total, *refs):
     (
-        features_ref, backbone_ref, table_ref, text_ref, hits_ref, vectors_ref, weight_ref, linear_ref, planar_ref,
-        rows_ref, cols_ref,
-    ) = refs[:11]
-    ins = refs[11 : 11 + count]
-    proj_ref, merged_ref, probs_ref, lefts_ref, start_ref, normal_ref, scale_ref = refs[11 + count : 18 + count]
+        features_ref, backbone_ref, table_ref, text_ref, hits_ref, packed_ref, weight_ref, rows_ref, cols_ref,
+    ) = refs[:9]
+    ins = refs[9 : 9 + count]
+    (
+        proj_ref, merged_ref, probs_ref, lefts_ref, start_ref, normal_ref, scale_ref, vectors_ref, bias_ref,
+    ) = refs[9 + count : 18 + count]
     outs = refs[18 + count : 18 + 2 * count]
-    box_ref, conv_ref, local_ref, pooled_ref = refs[18 + 2 * count : 22 + 2 * count]
-    rest = refs[22 + 2 * count :]
+    box_ref, conv_ref, local_ref, pooled_ref, linear_ref, planar_ref = refs[18 + 2 * count : 24 + 2 * count]
+    rest = refs[24 + 2 * count :]
     rows = features_ref.shape[0]
     sums = exchange_stages(line, partial(pool_statistics, float(rows)), local_ref, pooled_ref, rest[:7])
     stages = gather_stages(line, ins, outs, rest[7:])
@@ -829,6 +1107,7 @@
         local_ref[1] = jnp.sum(center * center, axis=0, keepdims=True)
         sums.near()
         stages.start()
+        unpack(packed_ref, vectors_ref, bias_ref, linear_ref, planar_ref)
         make_boxes(rows_ref, cols_ref, box_ref)
         text_start = jnp.where(hit_rows(0), vector(2), text_ref[...].astype(jnp.float32))
         start_ref[...] = text_start
@@ -887,8 +1166,8 @@
 
 
 def forward_layer(
-    features, backbone, table, text, hits, vectors, weights, linear_ext, planar_rows, anchor_rows, anchor_cols,
-    shards, token_total, collective_id,
+    features, backbone, table, text, hits, packed, weights, anchor_rows, anchor_cols, shards, token_total,
+    collective_id,
 ):
     dp = lax.axis_size("dp")
     line = dp // RING
@@ -915,6 +1194,8 @@
         (page, f32, whole(page)),
         (page, f32, whole(page)),
         ((8, MODEL_WIDTH), f32, whole((8, MODEL_WIDTH))),
+        ((16, MODEL_WIDTH), f32, whole((16, MODEL_WIDTH))),
+        ((CHUNKS, 1, MODEL_WIDTH), f32, whole((CHUNKS, 1, MODEL_WIDTH))),
         *(((2 * dp, *shard.shape), shard.dtype, anywhere) for shard in shards),
     ]
     pool = (2, 1, MODEL_WIDTH)
@@ -927,10 +1208,8 @@
             once(table.shape),
             once(text.shape),
             once(hits.shape),
-            once(vectors.shape),
+            once(packed.shape),
             pl.BlockSpec((MODEL_WIDTH, MODEL_WIDTH), lambda i: (0, column_at_step(i))),
-            once(linear_ext.shape),
-            once(planar_rows.shape),
             once(anchor_rows.shape),
             once(anchor_cols.shape),
             *[anywhere] * count,
@@ -942,6 +1221,8 @@
             pltpu.VMEM(page, f32),
             pltpu.VMEM(pool, f32),
             pltpu.VMEM(pool, f32),
+            pltpu.VMEM((HEADS, 1, 2 * PAGE_TOKENS), f32),
+            pltpu.VMEM((HEADS, 1, SP_B), f32),
             *exchange_scratch(line, pool),
             *gather_sems(line, count),
         ],
@@ -950,8 +1231,7 @@
         ),
         name="forward_layer",
     )(
-        features, backbone, table, text, hits, vectors, weights, linear_ext, planar_rows, anchor_rows, anchor_cols,
-        *shards,
+        features, backbone, table, text, hits, packed, weights, anchor_rows, anchor_cols, *shards,
     )
 
 
@@ -1133,15 +1413,17 @@
 
 def last_kernel(line, count, token_total, *refs):
     sums_ref, kept_ref, normal_ref, scale_ref, features_ref, backbone_ref = refs[:6]
-    ins = refs[6 : 6 + count]
-    feature_grad_ref, total_ref = refs[6 + count : 8 + count]
-    outs = refs[8 + count : 9 + 2 * count]
-    turned_ref, conv_grad_ref, late_ref = refs[9 + 2 * count : 12 + 2 * count]
-    rest = refs[12 + 2 * count :]
-    sums = exchange_stages(line, add_up, sums_ref, total_ref, rest[:7])
-    early_scratch = 5 * count + 9
-    early = scatter_stages(line, ins, outs[:count], rest[7 : 7 + early_scratch])
-    late = scatter_stages(line, [late_ref], outs[count:], rest[7 + early_scratch :])
+    ins = refs[6 : 7 + count]
+    feature_grad_ref, total_ref = refs[7 + count : 9 + count]
+    outs = refs[9 + count : 11 + 2 * count]
+    turned_ref, conv_grad_ref, late_ref = refs[11 + 2 * count : 14 + 2 * count]
+    rest = refs[14 + 2 * count :]
+    local_ref, *rest = rest
+    sums = exchange_stages(line, add_up, local_ref, total_ref, rest[:7])
+    stop = 7 + 5 * count + 9
+    early = scatter_stages(line, ins[:count], outs[:count], rest[7:stop])
+    late = scatter_stages(line, [late_ref], outs[count : count + 1], rest[stop : stop + 14])
+    flat = flat_scatter_stages(line, ins[count:], outs[count + 1 :], rest[stop + 14 :])
     share = late_ref.shape[2]
 
     def first(stages, k):
@@ -1154,17 +1436,21 @@
         spread(line, 4, k, 0, stages.third)
 
     greet_peers(line)
+    local_ref[...] = sums_ref[2:4, :]
     sums.near()
+    flat.start()
     early.start()
+    sums.far()
+    first(flat, 0)
     first(early, 0)
-    sums.far()
     first(early, 1)
     sums.total()
     conv_grad_ref[...] = (
-        scale_ref[...]
+        scale_ref[0:1, :]
         * (kept_ref[...] - total_ref[0:1, :] / token_total - normal_ref[...] * (total_ref[1:2, :] / token_total))
     ).astype(jnp.bfloat16)
     second(early, 0)
+    first(flat, 1)
     first(early, 2)
     first(early, 3)
 
@@ -1187,6 +1473,7 @@
     late.start()
     for k in range(4):
         first(late, k)
+    first(flat, 2)
     second(early, 1)
     third(early, 0)
 
@@ -1196,46 +1483,56 @@
         return unused
 
     lax.fori_loop(0, features_ref.shape[1] // 512, feature, 0)
+    first(flat, 3)
     second(early, 2)
     for k in range(4):
         second(late, k)
+    flat.second()
     second(early, 3)
     third(early, 1)
     third(early, 2)
     for k in range(3):
         third(late, k)
+    flat.third()
     third(early, 3)
     third(late, 3)
     sums.end()
     early.end()
     late.end()
-
-
-def last_layer(sums, kept, normal, scale, features, backbone, grads, token_total, collective_id):
+    flat.end()
+
+
+def last_layer(
+    sums, kept, normal, scale, features, backbone, grads, flat_grad, token_total, collective_id
+):
     dp = lax.axis_size("dp")
     line = dp // RING
     count = len(grads)
     blocks = [(grad.shape[1:], grad.dtype) for grad in grads]
+    flat = [(flat_grad.shape[1:], flat_grad.dtype)]
+    pair = (2, MODEL_WIDTH)
     channels = backbone.shape[0]
     late = [((channels // (2 * dp), MODEL_WIDTH), jnp.bfloat16)]
     anywhere = pl.BlockSpec(memory_space=pl.ANY)
     vmem = pl.BlockSpec(memory_space=pltpu.VMEM)
     return pl.pallas_call(
         partial(last_kernel, line, count, float(token_total)),
-        in_specs=[*[vmem] * 6, *[anywhere] * count],
-        out_specs=[vmem] * (3 + count),
+        in_specs=[*[vmem] * 6, *[anywhere] * (count + 1)],
+        out_specs=[vmem] * (4 + count),
         out_shape=[
             jax.ShapeDtypeStruct(features.shape, jnp.float32),
-            jax.ShapeDtypeStruct(sums.shape, jnp.float32),
-            *(jax.ShapeDtypeStruct(shape, jnp.float32) for shape, kind in blocks + late),
+            jax.ShapeDtypeStruct(pair, jnp.float32),
+            *(jax.ShapeDtypeStruct(shape, jnp.float32) for shape, kind in blocks + late + flat),
         ],
         scratch_shapes=[
             pltpu.VMEM((channels, PAGE_TOKENS), jnp.bfloat16),
             pltpu.VMEM(kept.shape, jnp.bfloat16),
             pltpu.VMEM((dp, 2, *late[0][0]), jnp.bfloat16),
-            *exchange_scratch(line, sums.shape),
+            pltpu.VMEM(pair, jnp.float32),
+            *exchange_scratch(line, pair),
             *scatter_scratch(line, blocks),
             *scatter_scratch(line, late),
+            *flat_scatter_scratch(line, flat),
         ],
         compiler_params=pltpu.CompilerParams(
             collective_id=collective_id, has_side_effects=True, vmem_limit_bytes=63 << 20
@@ -1243,8 +1540,62 @@
         name="last_layer",
     )(
         sums, kept, normal, scale, features, backbone,
-        *(grad.reshape(line * RING, 2, *grad.shape[1:]) for grad in grads),
-    )
+        *(grad.reshape(line * RING, 2, *grad.shape[1:]) for grad in [*grads, flat_grad]),
+    )
+
+
+def finish_kernel(count, share, expand_share, bias_rows, *refs):
+    ins = refs[:count]
+    small_ref, total_ref = refs[count : count + 2]
+    outs = refs[count + 2 : 2 * count + 2]
+    small_outs = refs[2 * count + 2 : 2 * count + 14]
+    staged = refs[2 * count + 14 : 2 * count + 26]
+    sems, small_sems = refs[2 * count + 26 :]
+    copies = [pltpu.make_async_copy(ins[k], outs[k], sems.at[k]) for k in range(count)]
+    for copy in copies:
+        copy.start()
+    staged[0][...] = small_ref[:bias_rows, :HEADS]
+    staged[1][...] = small_ref[bias_rows : 2 * bias_rows, :HEADS]
+    for k in range(7):
+        staged[2 + k][...] = small_ref[2 * bias_rows + k : 2 * bias_rows + k + 1, :share]
+    staged[9][...] = small_ref[2 * bias_rows + 7 : 2 * bias_rows + 8, :expand_share]
+    owner = (lax.axis_index("dp") * 2 + lax.axis_index("pair")) * share
+    chosen = lax.broadcasted_iota(jnp.int32, (MODEL_WIDTH, 128), 0) == (
+        lax.broadcasted_iota(jnp.int32, (MODEL_WIDTH, 128), 1) + owner
+    )
+    owned = lax.dot_general(
+        total_ref[...], chosen.astype(jnp.float32), (((1,), (0,)), ((), ())),
+        precision=lax.Precision.HIGHEST, preferred_element_type=jnp.float32,
+    )
+    for k in range(2):
+        staged[10 + k][...] = owned[k : k + 1, :share]
+    small_copies = [pltpu.make_async_copy(staged[k], small_outs[k], small_sems.at[k]) for k in range(12)]
+    for copy in small_copies:
+        copy.start()
+    for copy in copies + small_copies:
+        copy.wait()
+
+
+def finish(arrays, small, totals, share, expand_share, bias_rows):
+    count = len(arrays)
+    anywhere = pl.BlockSpec(memory_space=pl.ANY)
+    vmem = pl.BlockSpec(memory_space=pltpu.VMEM)
+    shapes = [(bias_rows, HEADS)] * 2 + [(1, share)] * 7 + [(1, expand_share)] + [(1, share)] * 2
+    return pl.pallas_call(
+        partial(finish_kernel, count, share, expand_share, bias_rows),
+        in_specs=[vmem] * (count + 2),
+        out_specs=[anywhere] * (count + 12),
+        out_shape=[
+            *(jax.ShapeDtypeStruct(array.shape, array.dtype) for array in arrays),
+            *(jax.ShapeDtypeStruct(shape, jnp.float32) for shape in shapes),
+        ],
+        scratch_shapes=[
+            *(pltpu.VMEM(shape, jnp.float32) for shape in shapes),
+            pltpu.SemaphoreType.DMA((count,)),
+            pltpu.SemaphoreType.DMA((12,)),
+        ],
+        name="finish",
+    )(*arrays, small, totals)
 
 
 norm_epsilon = 1e-05
@@ -1263,9 +1614,6 @@
         - jnp.mean(scaled, axis=-1, keepdims=True)
         - normal * jnp.mean(scaled * normal, axis=-1, keepdims=True)
     )
-
-
-CHUNKS = 4
 
 
 def mixer_kernel(
@@ -1398,10 +1746,15 @@
 
 
 def padded_rows(pieces):
-    rows = [jnp.pad(piece.astype(jnp.float32), ((0, 0), (0, 128 - piece.shape[1]))) for piece in pieces]
     total = sum(piece.shape[0] for piece in pieces)
-    rows.append(jnp.zeros((-total % 8, 128), jnp.float32))
-    return jnp.concatenate(rows, axis=0)
+    rows = -(-total // 8) * 8
+    whole = jnp.zeros((rows, 128), jnp.float32)
+    start = 0
+    for piece in pieces:
+        stop = start + piece.shape[0]
+        whole += jnp.pad(piece.astype(jnp.float32), ((start, rows - stop), (0, 128 - piece.shape[1])))
+        start = stop
+    return whole
 
 
 def blocks_of(grad, devices):
@@ -1442,20 +1795,14 @@
     share = MODEL_WIDTH // devices
     expand_share = expand_bias.shape[0]
     bias_rows = REL_B // devices
-    vectors = jnp.stack(
-        [
-            batch_gain, batch_shift, text_blank, region_blank, mixer_gain, mixer_shift, reduce_bias,
-            output_gain, output_shift,
-        ]
-    )
-    small = padded_rows([linear_bias, planar_bias, vectors, expand_bias[None, :]])
-    packed, w_backbone, w_table, w_stream = gather_all(
-        (small, backbone_weight, position_table, stream_weights), 0
-    )
-    w_linear = packed[:, :bias_rows, :HEADS].reshape(REL_B, HEADS)
-    w_planar = packed[:, bias_rows : 2 * bias_rows, :HEADS].reshape(SP_B, HEADS)
-    w_vectors = packed[:, 2 * bias_rows : 2 * bias_rows + 9, :share].transpose(1, 0, 2).reshape(9, -1)
-    w_expand_bias = packed[:, 2 * bias_rows + 9, :expand_share].reshape(-1)
+    vectors = (
+        batch_gain, batch_shift, text_blank, region_blank, mixer_gain, mixer_shift, reduce_bias,
+        output_gain, output_shift, expand_bias,
+    )
+    small = padded_rows([linear_bias, planar_bias, *(vector[None, :] for vector in vectors)])
+    packed, w_backbone, w_stream, w_table = gather_all(
+        (small, backbone_weight, stream_weights), (position_table,), 0
+    )
     w_backbone, w_table, w_stream = (
         whole.reshape(-1, whole.shape[-1]) for whole in (w_backbone, w_table, w_stream)
     )
@@ -1463,17 +1810,16 @@
     anchor_rows = jnp.concatenate([text_anchors, region_anchors], axis=0)
     anchor_cols = anchor_rows.T
     hits = jnp.stack([text_masked, region_masked], axis=1)
-    proj, merged_low, probs, lefts, start_sum, normal_feat, batch_scale, *wholes = forward_layer(
-        region_features, w_backbone, w_table, text_inputs, hits, w_vectors, w_stream, linear_extended(w_linear),
-        w_planar.T[:, None, :], anchor_rows, anchor_cols, (merge_weight, expand_weight, reduce_weight),
-        token_total, 4,
+    proj, merged_low, probs, lefts, start_sum, normal_feat, batch_scale, w_vectors, w_expand_bias, *wholes = forward_layer(
+        region_features, w_backbone, w_table, text_inputs, hits, packed, w_stream, anchor_rows, anchor_cols,
+        (merge_weight, expand_weight, reduce_weight), token_total, 4,
     )
     w_merge, w_expand, w_reduce = (whole.reshape(-1, whole.shape[-1]) for whole in wholes)
     (
         layer_output, mixer_in_grad, merged_grad, merge_weight_grad, expand_weight_grad, reduce_weight_grad,
         mixer_sums, expand_bias_grad,
     ) = mixer_layer(
-        merged_low, start_sum, cotangent, w_vectors, w_expand_bias.reshape(CHUNKS, 1, -1),
+        merged_low, start_sum, cotangent, w_vectors, w_expand_bias,
         w_merge, w_expand, w_reduce,
     )
     early = (expand_weight_grad, reduce_weight_grad, merge_weight_grad)
@@ -1484,9 +1830,6 @@
         proj, probs, merged_grad, anchor_rows, anchor_cols, lefts, w_stream, mixer_in_grad, normal_feat, hits,
         [blocks_of(grad, devices) for grad in early], 5,
     )
-    expand_weight_grad, reduce_weight_grad, merge_weight_grad = (
-        part.reshape(-1, grad.shape[1]) for part, grad in zip(early_shares, early)
-    )
     vector_grads = jnp.concatenate([start_sums[:2], mixer_sums[:5]], axis=0)
     pieces = [
         linear_folded(linear_sums[:, 0]).T.reshape(devices, bias_rows, HEADS),
@@ -1494,44 +1837,45 @@
         vector_grads.reshape(7, devices, share).transpose(1, 0, 2),
         expand_bias_grad.reshape(devices, 1, expand_share),
     ]
-    small_grads = jax.vmap(lambda *parts: padded_rows(parts))(*pieces)
-    late = (stream_weights_grad, position_table_grad)
-    feature_gradient, totals, small, *shares = last_layer(
-        start_sums[2:4], region_kept, normal_feat, batch_scale[:1], region_features,
-        w_backbone, [small_grads, *(blocks_of(grad, devices) for grad in late)], token_total, 1,
-    )
-    stream_weights_grad, position_table_grad = (
-        part.reshape(-1, grad.shape[1]) for part, grad in zip(shares, late)
-    )
-    backbone_weight_grad = shares[2]
-    owned = lax.dynamic_slice_in_dim(totals, lax.axis_index(AXES) * share, share, axis=1)
-    batch_shift_gradient = owned[0]
-    batch_gain_gradient = owned[1]
-    vector_shares = small[2 * bias_rows : 2 * bias_rows + 7, :share]
+    rows = sum(piece.shape[1] for piece in pieces)
+    pieces = [jnp.pad(piece, ((0, 0), (0, 0), (0, 128 - piece.shape[2]))) for piece in pieces]
+    small_grads = jnp.pad(jnp.concatenate(pieces, axis=1), ((0, 0), (0, -rows % 8), (0, 0)))
+    feature_gradient, totals, small, stream_share, backbone_weight_grad, table_share = last_layer(
+        start_sums, region_kept, normal_feat, batch_scale, region_features, w_backbone,
+        [small_grads, blocks_of(stream_weights_grad, devices)], blocks_of(position_table_grad, devices),
+        token_total, 1,
+    )
+    arrays = (
+        text_gradient, feature_gradient, backbone_weight_grad, table_share, stream_share, *early_shares,
+    )
+    (
+        text_gradient, feature_gradient, backbone_weight_grad, table_share, stream_share, expand_share_grad,
+        reduce_share_grad, merge_share_grad, linear_grad, planar_grad, *vector_grads,
+    ) = finish(arrays, small, totals, share, expand_share, bias_rows)
+    vector_grads = [grad.reshape(-1) for grad in vector_grads]
     return (
         layer_output,
         text_gradient,
         feature_gradient,
         backbone_weight_grad,
-        batch_gain_gradient,
-        batch_shift_gradient,
-        vector_shares[0],
-        vector_shares[1],
-        position_table_grad,
-        stream_weights_grad,
-        small[:bias_rows, :HEADS],
-        small[bias_rows : 2 * bias_rows, :HEADS],
-        merge_weight_grad,
-        vector_shares[2],
-        vector_shares[3],
-        expand_weight_grad,
-        small[2 * bias_rows + 7, :expand_share],
-        reduce_weight_grad,
-        vector_shares[4],
-        vector_shares[5],
-        vector_shares[6],
-    )
-
+        vector_grads[9],
+        vector_grads[8],
+        vector_grads[0],
+        vector_grads[1],
+        table_share.reshape(-1, position_table.shape[1]),
+        stream_share.reshape(-1, stream_weights.shape[1]),
+        linear_grad,
+        planar_grad,
+        merge_share_grad.reshape(-1, MODEL_WIDTH),
+        vector_grads[2],
+        vector_grads[3],
+        expand_share_grad.reshape(-1, expand_weight.shape[1]),
+        vector_grads[7],
+        reduce_share_grad.reshape(-1, MODEL_WIDTH),
+        vector_grads[4],
+        vector_grads[5],
+        vector_grads[6],
+    )
 
 def solution(mesh):
     in_specs = (

time: 358 us -> 326 us (0.911)
  local copies, waits for them, and re-layouts: 30.8 us -> 4.48 us
    unnamed x31 -> x9, local copies, waits for them, and re-layouts: 9.31 us -> 0.95 us
    slice x4 -> x0, local copies, waits for them, and re-layouts: 3.74 us -> none  [the longest x1 1.32 us: per_device(): batch_scale[:1]]
    pallas_call x1, Pallas kernels: 60 us -> 63.7 us  [forward_layer(): pl.pallas_call(partial(forward_kernel, line, count, float(token_total)),...]
    pallas_call x1 -> x2, Pallas kernels: 84 us -> 80.4 us  [the longest x1 75.7 us: gather_all(): pl.pallas_call(partial(gather_kernel, line, count, flat), in_specs=[pl.Bl...]
where the time goes in v1:
time: 326 us; the launch traced here: 325 us
  Pallas kernels  315 us (97%)
  local copies, waits for them, and re-layouts  4.48 us (1%)
  other arithmetic  4.09 us (1%)
    pallas_call x1, Pallas kernels, last_layer(): pl.pallas_call(partial(last_kernel, line, count, float(token_total)), in_...  87.3 us
    pallas_call x1, Pallas kernels, gather_all(): pl.pallas_call(partial(gather_kernel, line, count, flat), in_specs=[pl.Bl...  75.7 us
    pallas_call x1, Pallas kernels, forward_layer(): pl.pallas_call(partial(forward_kernel, line, count, float(token_total)),...  63.7 us
    pallas_call x1, Pallas kernels, backward_layer(): pl.pallas_call(partial(backward_kernel, line, count), grid=(TABLE_STEP +...  62.8 us
    pallas_call x1, Pallas kernels, mixer_layer(): pl.pallas_call(mixer_kernel, grid=(2 * CHUNKS,), in_specs=[once(page), on...  20.9 us

profile of v1, /device:TPU:8, one launch (start us, length us, event | category | flops | bytes accessed | tf_op | source)
XLA Modules:
  0.0 324.7 jit_solution(17174447379779401964)
XLA Ops:
  0.7 0.7 pad_add_fusion.1
  1.4 0.7 pad_add_fusion.refs_7_.refs_3_
  2.1 0.0 copy-start
  2.1 1.4 convert_add_fusion.refs_0_
  3.5 0.8 copy.68.refs_4_.refs_9_
  4.3 0.8 copy.67
  5.1 75.7 %gather_all.1 = (f32[32,32,128]{2,1,0:T(8,128)}, bf16[32,64,768]{2,1,0:T(8,128)(2,1)}, bf16[32,24,7680]{2,1,0:T(8,128)(2,1)}, bf16[16,2,32,1536]{3,2,1,0:T(8,128)(2,1)}) custom-call(f32[32,128]{1,0:T(8,128)} %convert_add_fusion.refs_0_, bf16[64,768]{1,0:T(8,128)(2,1)} %refs_1_.1, bf16[24,7680]{1,0:T(8,128)(2,1)} %refs_2_.1, bf16[32,1536]{1,0:T(8,128)(2,1)} %refs_3_.2), custom_call_target="tpu_custom_call" | custom-call | tf_op jit(solution)/shard_map/gather_all/pallas_call | solution.py:549
  80.8 0.0 copy-done
  80.8 63.7 %forward_layer.1 = (bf16[256,7680]{1,0:T(8,128)(2,1)}, bf16[256,768]{1,0:T(8,128)(2,1)}, f32[2,12,256,256]{3,2,1,0:T(8,128)}, bf16[4,256,768]{2,1,0:T(8,128)(2,1...) custom-call(bf16[256,2048]{1,0:T(8,128)(2,1)} %refs_4_.1, ...), custom_call_target="tpu_custom_call" | custom-call | tf_op jit(solution)/shard_map/forward_layer/pallas_call | solution.py:1202
  144.6 20.9 %mixer_layer.1 = (bf16[256,768]{1,0:T(8,128)(2,1)}, f32[256,768]{1,0:T(8,128)}, bf16[256,768]{1,0:T(8,128)(2,1)}, bf16[768,768]{1,0:T(8,128)(2,1)}, bf16[768,307...) custom-call(bf16[256,768]{1,0:T(8,128)(2,1)} %get-tuple-element.85.merged_ref, ...), custom_call_target="tpu_custom_call" | custom-call | tf_op jit(solution)/shard_map/mixer_layer/pallas_call | solution.py:1714
  165.5 0.0 copy-start.1
  165.5 0.0 copy-start.2
  165.5 62.8 %backward_layer.1 = (f32[12,1,512]{2,1,0:T(1,128)}, f32[12,1,256]{2,1,0:T(1,128)}, bf16[768,7680]{1,0:T(8,128)(2,1)}, bf16[1024,1536]{1,0:T(8,128)(2,1)}, f32[25...) custom-call(bf16[256,7680]{1,0:T(8,128)(2,1)} %get-tuple-element.93., ...), custom_call_target="tpu_custom_call" | custom-call | tf_op jit(solution)/shard_map/backward_layer/pallas_call | solution.py:1358
  228.4 0.7 slice.18
  229.1 0.0 copy-done.1
  229.1 0.0 copy-done.2
  229.2 0.1 reshape.130
  229.3 0.7 copy.85
  230.0 0.2 slice_reduce_fusion
  230.2 0.1 slice_reduce_fusion.1
  230.3 0.1 copy.70
  230.4 0.1 copy.71
  230.5 0.1 maximum_bitcast_fusion
  230.6 0.1 reshape.129
  230.7 0.1 copy.80
  230.8 0.1 copy.81
  230.9 0.8 copy.83
  231.7 0.8 select_maximum_fusion
  232.5 87.3 %last_layer.1 = (f32[256,2048]{1,0:T(8,128)}, f32[2,768]{1,0:T(2,128)}, f32[24,128]{1,0:T(8,128)}, f32[24,7680]{1,0:T(8,128)}, f32[64,768]{1,0:T(8,128)}, /*index=5*/f32[32,1536]{1,0:T(8,128)}) custom-call(f32[8,768]{1,0:T(8,128)} %get-tuple-element.103.refs_0_, f32[256,768]{1,0:T(8,128)} %get-tuple-element.104.refs_1_, ...), custom_call_target="tpu_custom_call" | custom-call | tf_op jit(solution)/shard_map/last_layer/pallas_call | solution.py:1518
  319.9 4.7 %finish.1 = (f32[256,768]{1,0:T(8,128)}, f32[256,2048]{1,0:T(8,128)}, f32[64,768]{1,0:T(8,128)}, f32[32,1536]{1,0:T(8,128)}, f32[24,7680]{1,0:T(8,128)}, /*index...) custom-call(f32[256,768]{1,0:T(8,128)} %get-tuple-element.102.refs_0, ...), custom_call_target="tpu_custom_call" | custom-call | tf_op jit(solution)/shard_map/finish/pallas_call | solution.py:1584
  (3 shorter events, 0.1 us)
Async XLA Ops:
  2.1 78.8 %copy-start = (s32[4,256]{1,0:T(4,128)}, s32[4,256]{1,0:T(4,128)S(1)}, u32[]{:S(2)}) copy-start(s32[4,256]{1,0:T(4,128)S(1)} %pad_add_fusion.refs_7_.refs_3_) | copy-start | bytes 12292
  165.5 63.6 %copy-start.1 = (f32[8,768]{1,0:T(8,128)S(1)}, f32[8,768]{1,0:T(8,128)}, u32[]{:S(2)}) copy-start(f32[8,768]{1,0:T(8,128)} %get-tuple-element.108) | copy-start | bytes 73732
  165.5 63.6 %copy-start.2 = (f32[4,1,768]{2,1,0:T(1,128)S(1)}, f32[4,1,768]{2,1,0:T(1,128)}, u32[]{:S(2)}) copy-start(f32[4,1,768]{2,1,0:T(1,128)} %get-tuple-element.109) | copy-start | bytes 36868

commit v2 on v1

--- a/solution.py
+++ b/solution.py
@@ -140,11 +140,8 @@
                 )
             )
             parts = jnp.concatenate([grad_logits * mask_ref[stream, side] for side in range(4)], axis=1)
-            placed = dot_nn(parts, place_ref[stream])
-            placed_high = placed.astype(jnp.bfloat16)
-            placed_low = (placed - placed_high.astype(jnp.float32)).astype(jnp.bfloat16)
-            turned = turned_ref[stream]
-            cells = dot_nn(turned, placed_high) + dot_nn(turned, placed_low)
+            placed = dot_nn(parts, place_ref[stream]).astype(jnp.bfloat16)
+            cells = dot_nn(turned_ref[stream], placed)
             sums = jnp.sum(
                 pltpu.roll(cells, SP_B - SP_SIDE // 2, 1, stride=1, stride_axis=0), axis=0, keepdims=True
             )
@@ -275,16 +272,19 @@
             src, block(a, zz, qq), c_send.at[a, zz * RING + qq], c_recv.at[a, zz * RING + qq], z, q, 1 - c
         )
 
-    def start():
+    def start_line():
         for a in range(count):
             own(a).start()
             for way in range(2):
                 @pl.when(z < line - 1 if way == 0 else z > 0)
                 def _():
                     z_copy(a, way, 0, True).start()
+            c_copy(a, z, q, True).start()
+
+    def start_ring():
+        for a in range(count):
             for axis in range(2):
                 xy_copy(a, axis, z, True).start()
-            c_copy(a, z, q, True).start()
 
     def arrived(a, zz):
         for axis in range(2):
@@ -376,7 +376,9 @@
             own(a).wait()
         lax.fori_loop(0, line, drain, 0)
 
-    return SimpleNamespace(start=start, along=along, around=around, home=home, end=end)
+    return SimpleNamespace(
+        start_line=start_line, start_ring=start_ring, along=along, around=around, home=home, end=end
+    )
 
 
 def gather_sems(line, count):
@@ -514,30 +516,48 @@
     plane = flat_gather_stages(line, ins[count:], outs[count:], sems[9:])
     greet(line)
     plane.start()
-    stages.start()
-    plane.around()
-    plane.home()
+    stages.start_line()
+    stages.start_ring()
 
     def generation(g, unused):
-        @pl.when(jnp.logical_and(g >= 2, g <= line))
+        stages.along(g)
+        stages.around(g - 1)
+
+        @pl.when(g == 1)
         def _():
-            plane.along(g - 1)
-
+            plane.around()
+
+        @pl.when(g == 2)
+        def _():
+            plane.home()
+
+        @pl.when(g >= 3)
+        def _():
+            stages.home(g - 3)
+
+        return unused
+
+    lax.fori_loop(1, line, generation, 0)
+    if line == 2:
+        plane.home()
+
+    def rest(g, unused):
         @pl.when(g <= line - 1)
         def _():
-            stages.along(g)
-
-        @pl.when(g <= line)
+            plane.along(g)
+
+        @pl.when(g == 1)
         def _():
-            stages.around(g - 1)
-
-        @pl.when(g >= 2)
+            stages.around(line - 1)
+
+        @pl.when(g + line - 4 >= 0)
         def _():
-            stages.home(g - 2)
+            stages.home(g + line - 4)
 
         return unused
 
-    lax.fori_loop(1, line + 2, generation, 0)
+    lax.fori_loop(1, 4, rest, 0)
+    lax.fori_loop(4, line, lambda g, unused: (plane.along(g), unused)[1], 0)
     stages.end()
     plane.end()
 
@@ -1076,7 +1096,7 @@
 
 def forward_kernel(line, count, token_total, *refs):
     (
-        features_ref, backbone_ref, table_ref, text_ref, hits_ref, packed_ref, weight_ref, rows_ref, cols_ref,
+        features_ref, backbone_hbm, table_hbm, text_ref, hits_ref, packed_ref, weight_ref, rows_ref, cols_ref,
     ) = refs[:9]
     ins = refs[9 : 9 + count]
     (
@@ -1084,7 +1104,7 @@
     ) = refs[9 + count : 18 + count]
     outs = refs[18 + count : 18 + 2 * count]
     box_ref, conv_ref, local_ref, pooled_ref, linear_ref, planar_ref = refs[18 + 2 * count : 24 + 2 * count]
-    rest = refs[24 + 2 * count :]
+    backbone_ref, table_ref, fetch_sem, *rest = refs[24 + 2 * count :]
     rows = features_ref.shape[0]
     sums = exchange_stages(line, partial(pool_statistics, float(rows)), local_ref, pooled_ref, rest[:7])
     stages = gather_stages(line, ins, outs, rest[7:])
@@ -1098,7 +1118,15 @@
 
     @pl.when(step == 0)
     def _():
+        fetches = [
+            pltpu.make_async_copy(source, target, fetch_sem.at[k])
+            for k, (source, target) in enumerate(((backbone_hbm, backbone_ref), (table_hbm, table_ref)))
+        ]
+        for fetch in fetches:
+            fetch.start()
         greet_peers(line)
+        stages.start_line()
+        fetches[0].wait()
         conv = dot_nn(features_ref[...], backbone_ref[...])
         mean = jnp.mean(conv, axis=0, keepdims=True)
         center = conv - mean
@@ -1106,13 +1134,14 @@
         local_ref[0] = mean
         local_ref[1] = jnp.sum(center * center, axis=0, keepdims=True)
         sums.near()
-        stages.start()
+        stages.start_ring()
         unpack(packed_ref, vectors_ref, bias_ref, linear_ref, planar_ref)
         make_boxes(rows_ref, cols_ref, box_ref)
         text_start = jnp.where(hit_rows(0), vector(2), text_ref[...].astype(jnp.float32))
         start_ref[...] = text_start
         lefts_ref[0] = text_start.astype(jnp.bfloat16)
         coords = lax.broadcasted_iota(jnp.int32, (rows, COORDS), 1)
+        fetches[1].wait()
         for stream in range(2):
             space = None
             for axis in range(2):
@@ -1155,8 +1184,8 @@
 
     at_steps(
         [
-            (3, [along(0), around(0)]),
-            (10, [along(1)]),
+            (1, [along(0), around(0)]),
+            (8, [along(1)]),
             (11, [around(1)]),
             (13, [along(2), home(0)]),
             (15, [around(2), home(1)]),
@@ -1204,8 +1233,8 @@
         grid=(1 + KINDS + PAIRS,),
         in_specs=[
             once(features.shape),
-            once(backbone.shape),
-            once(table.shape),
+            anywhere,
+            anywhere,
             once(text.shape),
             once(hits.shape),
             once(packed.shape),
@@ -1223,6 +1252,9 @@
             pltpu.VMEM(pool, f32),
             pltpu.VMEM((HEADS, 1, 2 * PAGE_TOKENS), f32),
             pltpu.VMEM((HEADS, 1, SP_B), f32),
+            pltpu.VMEM(backbone.shape, bf16),
+            pltpu.VMEM(table.shape, bf16),
+            pltpu.SemaphoreType.DMA((2,)),
             *exchange_scratch(line, pool),
             *gather_sems(line, count),
         ],
@@ -1258,6 +1290,7 @@
         greet(line)
         stages.start()
         make_places(rows_ref, cols_ref, *helpers)
+        spread(line, 4, 0, 0, stages.first)
 
     def first(k):
         return lambda: spread(line, 4, k, 0, stages.first)
@@ -1269,14 +1302,14 @@
         return lambda: spread(line, 4, k, 0, stages.third)
 
     slots = {
-        1: [first(0)],
-        3: [first(1)],
-        7: [second(0)],
-        8: [first(2)],
-        10: [first(3)],
-        12: [second(1)],
-        17: [third(0)],
-        22: [second(2), second(3)],
+        1: [first(1)],
+        5: [second(0)],
+        6: [first(2)],
+        8: [first(3)],
+        10: [second(1)],
+        15: [third(0)],
+        19: [second(2)],
+        21: [second(3)],
     }
 
     def pump(sub):
@@ -1335,7 +1368,7 @@
                 sums_ref[3:4, :] = jnp.sum(kept * normal_ref[...], axis=0, keepdims=True)
 
     at_steps(
-        [(PAIRS + 3, [third(1)]), (PAIRS + 8, [third(2)]), (TABLE_STEP + 1, [third(3), stages.end])]
+        [(PAIRS, [third(1)]), (PAIRS + 7, [third(2)]), (TABLE_STEP + 1, [third(3), stages.end])]
     )
 
 
@@ -1412,13 +1445,13 @@
 
 
 def last_kernel(line, count, token_total, *refs):
-    sums_ref, kept_ref, normal_ref, scale_ref, features_ref, backbone_ref = refs[:6]
+    sums_ref, kept_ref, normal_ref, scale_ref, features_hbm, backbone_hbm = refs[:6]
     ins = refs[6 : 7 + count]
     feature_grad_ref, total_ref = refs[7 + count : 9 + count]
     outs = refs[9 + count : 11 + 2 * count]
     turned_ref, conv_grad_ref, late_ref = refs[11 + 2 * count : 14 + 2 * count]
     rest = refs[14 + 2 * count :]
-    local_ref, *rest = rest
+    features_ref, backbone_ref, fetch_sem, local_ref, *rest = rest
     sums = exchange_stages(line, add_up, local_ref, total_ref, rest[:7])
     stop = 7 + 5 * count + 9
     early = scatter_stages(line, ins[:count], outs[:count], rest[7:stop])
@@ -1435,11 +1468,17 @@
     def third(stages, k):
         spread(line, 4, k, 0, stages.third)
 
+    fetches = [
+        pltpu.make_async_copy(source, target, fetch_sem.at[k])
+        for k, (source, target) in enumerate(((features_hbm, features_ref), (backbone_hbm, backbone_ref)))
+    ]
     greet_peers(line)
     local_ref[...] = sums_ref[2:4, :]
     sums.near()
     flat.start()
     early.start()
+    for fetch in fetches:
+        fetch.start()
     sums.far()
     first(flat, 0)
     first(early, 0)
@@ -1454,6 +1493,9 @@
     first(early, 2)
     first(early, 3)
 
+    for fetch in fetches:
+        fetch.wait()
+
     def turn(k, unused):
         columns = pl.ds(pl.multiple_of(k * 512, 512), 512)
         turned_ref[columns, :] = features_ref[:, columns].T
@@ -1484,15 +1526,16 @@
 
     lax.fori_loop(0, features_ref.shape[1] // 512, feature, 0)
     first(flat, 3)
-    second(early, 2)
     for k in range(4):
         second(late, k)
+    second(early, 2)
     flat.second()
     second(early, 3)
     third(early, 1)
+    third(late, 0)
+    third(late, 1)
     third(early, 2)
-    for k in range(3):
-        third(late, k)
+    third(late, 2)
     flat.third()
     third(early, 3)
     third(late, 3)
@@ -1517,7 +1560,7 @@
     vmem = pl.BlockSpec(memory_space=pltpu.VMEM)
     return pl.pallas_call(
         partial(last_kernel, line, count, float(token_total)),
-        in_specs=[*[vmem] * 6, *[anywhere] * (count + 1)],
+        in_specs=[*[vmem] * 4, *[anywhere] * (count + 3)],
         out_specs=[vmem] * (4 + count),
         out_shape=[
             jax.ShapeDtypeStruct(features.shape, jnp.float32),
@@ -1528,6 +1571,9 @@
             pltpu.VMEM((channels, PAGE_TOKENS), jnp.bfloat16),
             pltpu.VMEM(kept.shape, jnp.bfloat16),
             pltpu.VMEM((dp, 2, *late[0][0]), jnp.bfloat16),
+            pltpu.VMEM(features.shape, jnp.bfloat16),
+            pltpu.VMEM(backbone.shape, jnp.bfloat16),
+            pltpu.SemaphoreType.DMA((2,)),
             pltpu.VMEM(pair, jnp.float32),
             *exchange_scratch(line, pair),
             *scatter_scratch(line, blocks),

time: 326 us -> 319 us (0.979)
  Pallas kernels: 315 us -> 309 us
where the time goes in v2:
time: 319 us
  Pallas kernels  309 us (97%)
  local copies, waits for them, and re-layouts  4.48 us (1%)
  other arithmetic  4.09 us (1%)
    pallas_call x1, Pallas kernels, last_layer(): pl.pallas_call(partial(last_kernel, line, count, float(token_total)), in_...  85 us
    pallas_call x1, Pallas kernels, gather_all(): pl.pallas_call(partial(gather_kernel, line, count, flat), in_specs=[pl.Bl...  75.1 us
    pallas_call x1, Pallas kernels, forward_layer(): pl.pallas_call(partial(forward_kernel, line, count, float(token_total)),...  62.5 us
    pallas_call x1, Pallas kernels, backward_layer(): pl.pallas_call(partial(backward_kernel, line, count), grid=(TABLE_STEP +...  61 us
    pallas_call x1, Pallas kernels, mixer_layer(): pl.pallas_call(mixer_kernel, grid=(2 * CHUNKS,), in_specs=[once(page), on...  20.9 us

profile of v2, /device:TPU:8, one launch (start us, length us, event | category | flops | bytes accessed | tf_op | source)
XLA Modules:
  0.0 318.6 jit_solution(8087821894485743762)
XLA Ops:
  0.7 0.7 pad_add_fusion.1
  1.4 0.7 pad_add_fusion.refs_7_.refs_3_
  2.1 0.0 copy-start
  2.1 1.4 convert_add_fusion.refs_0_
  3.5 0.8 copy.68.refs_4_.refs_9_
  4.3 0.8 copy.67
  5.1 75.1 %gather_all.1 = (f32[32,32,128]{2,1,0:T(8,128)}, bf16[32,64,768]{2,1,0:T(8,128)(2,1)}, bf16[32,24,7680]{2,1,0:T(8,128)(2,1)}, bf16[16,2,32,1536]{3,2,1,0:T(8,128)(2,1)}) custom-call(f32[32,128]{1,0:T(8,128)} %convert_add_fusion.refs_0_, bf16[64,768]{1,0:T(8,128)(2,1)} %refs_1_.1, bf16[24,7680]{1,0:T(8,128)(2,1)} %refs_2_.1, bf16[32,1536]{1,0:T(8,128)(2,1)} %refs_3_.2), custom_call_target="tpu_custom_call" | custom-call | tf_op jit(solution)/shard_map/gather_all/pallas_call | solution.py:569
  80.2 0.0 copy-done
  80.2 62.5 %forward_layer.1 = (bf16[256,7680]{1,0:T(8,128)(2,1)}, bf16[256,768]{1,0:T(8,128)(2,1)}, f32[2,12,256,256]{3,2,1,0:T(8,128)}, bf16[4,256,768]{2,1,0:T(8,128)(2,1...) custom-call(bf16[256,2048]{1,0:T(8,128)(2,1)} %refs_4_.1, ...), custom_call_target="tpu_custom_call" | custom-call | tf_op jit(solution)/shard_map/forward_layer/pallas_call | solution.py:1231
  142.7 20.9 %mixer_layer.1 = (bf16[256,768]{1,0:T(8,128)(2,1)}, f32[256,768]{1,0:T(8,128)}, bf16[256,768]{1,0:T(8,128)(2,1)}, bf16[768,768]{1,0:T(8,128)(2,1)}, bf16[768,307...) custom-call(bf16[256,768]{1,0:T(8,128)(2,1)} %get-tuple-element.85.merged_ref, ...), custom_call_target="tpu_custom_call" | custom-call | tf_op jit(solution)/shard_map/mixer_layer/pallas_call | solution.py:1760
  163.6 0.0 copy-start.1
  163.6 0.0 copy-start.2
  163.6 61.0 %backward_layer.1 = (f32[12,1,512]{2,1,0:T(1,128)}, f32[12,1,256]{2,1,0:T(1,128)}, bf16[768,7680]{1,0:T(8,128)(2,1)}, bf16[1024,1536]{1,0:T(8,128)(2,1)}, f32[25...) custom-call(bf16[256,7680]{1,0:T(8,128)(2,1)} %get-tuple-element.93., ...), custom_call_target="tpu_custom_call" | custom-call | tf_op jit(solution)/shard_map/backward_layer/pallas_call | solution.py:1391
  224.6 0.7 slice.18
  225.3 0.0 copy-done.1
  225.4 0.0 copy-done.2
  225.4 0.1 reshape.130
  225.5 0.7 copy.85
  226.2 0.2 slice_reduce_fusion
  226.4 0.1 slice_reduce_fusion.1
  226.5 0.1 copy.70
  226.6 0.1 copy.71
  226.7 0.1 maximum_bitcast_fusion
  226.8 0.1 reshape.129
  226.9 0.1 copy.80
  227.0 0.1 copy.81
  227.1 0.8 copy.83
  227.9 0.8 select_maximum_fusion
  228.7 85.0 %last_layer.1 = (f32[256,2048]{1,0:T(8,128)}, f32[2,768]{1,0:T(2,128)}, f32[24,128]{1,0:T(8,128)}, f32[24,7680]{1,0:T(8,128)}, f32[64,768]{1,0:T(8,128)}, /*index=5*/f32[32,1536]{1,0:T(8,128)}) custom-call(f32[8,768]{1,0:T(8,128)} %get-tuple-element.103.refs_0_, f32[256,768]{1,0:T(8,128)} %get-tuple-element.104.refs_1_, ...), custom_call_target="tpu_custom_call" | custom-call | tf_op jit(solution)/shard_map/last_layer/pallas_call | solution.py:1561
  313.8 4.7 %finish.1 = (f32[256,768]{1,0:T(8,128)}, f32[256,2048]{1,0:T(8,128)}, f32[64,768]{1,0:T(8,128)}, f32[32,1536]{1,0:T(8,128)}, f32[24,7680]{1,0:T(8,128)}, /*index...) custom-call(f32[256,768]{1,0:T(8,128)} %get-tuple-element.102.refs_0, ...), custom_call_target="tpu_custom_call" | custom-call | tf_op jit(solution)/shard_map/finish/pallas_call | solution.py:1630
  (3 shorter events, 0.1 us)
Async XLA Ops:
  2.1 78.1 %copy-start = (s32[4,256]{1,0:T(4,128)}, s32[4,256]{1,0:T(4,128)S(1)}, u32[]{:S(2)}) copy-start(s32[4,256]{1,0:T(4,128)S(1)} %pad_add_fusion.refs_7_.refs_3_) | copy-start | bytes 12292
  163.6 61.7 %copy-start.1 = (f32[8,768]{1,0:T(8,128)S(1)}, f32[8,768]{1,0:T(8,128)}, u32[]{:S(2)}) copy-start(f32[8,768]{1,0:T(8,128)} %get-tuple-element.108) | copy-start | bytes 73732
  163.6 61.7 %copy-start.2 = (f32[4,1,768]{2,1,0:T(1,128)S(1)}, f32[4,1,768]{2,1,0:T(1,128)}, u32[]{:S(2)}) copy-start(f32[4,1,768]{2,1,0:T(1,128)} %get-tuple-element.109) | copy-start | bytes 36868

commit v3 on v2

--- a/solution.py
+++ b/solution.py
@@ -1107,7 +1107,8 @@
     backbone_ref, table_ref, fetch_sem, *rest = refs[24 + 2 * count :]
     rows = features_ref.shape[0]
     sums = exchange_stages(line, partial(pool_statistics, float(rows)), local_ref, pooled_ref, rest[:7])
-    stages = gather_stages(line, ins, outs, rest[7:])
+    stages = gather_stages(line, ins[:-1], outs[:-1], rest[7:16])
+    plane = flat_gather_stages(line, ins[-1:], outs[-1:], rest[16:])
     step = pl.program_id(0)
 
     def vector(k):
@@ -1134,6 +1135,7 @@
         local_ref[0] = mean
         local_ref[1] = jnp.sum(center * center, axis=0, keepdims=True)
         sums.near()
+        plane.start()
         stages.start_ring()
         unpack(packed_ref, vectors_ref, bias_ref, linear_ref, planar_ref)
         make_boxes(rows_ref, cols_ref, box_ref)
@@ -1179,17 +1181,22 @@
     def around(k):
         return lambda: spread(line, 4, k, 0, stages.around)
 
+    def flat(k):
+        return lambda: spread(line, 3, k, 1, plane.along)
+
     def home(k):
         return lambda: spread(line, 4, k, 0, stages.home)
 
     at_steps(
         [
             (1, [along(0), around(0)]),
+            (5, [plane.around]),
             (8, [along(1)]),
-            (11, [around(1)]),
+            (11, [around(1), plane.home]),
             (13, [along(2), home(0)]),
+            (14, [flat(0)]),
             (15, [around(2), home(1)]),
-            (16, [around(3), home(2), home(3), sums.end, stages.end]),
+            (16, [flat(1), around(3), home(2), flat(2), home(3), sums.end, stages.end, plane.end]),
         ]
     )
 
@@ -1225,7 +1232,8 @@
         ((8, MODEL_WIDTH), f32, whole((8, MODEL_WIDTH))),
         ((16, MODEL_WIDTH), f32, whole((16, MODEL_WIDTH))),
         ((CHUNKS, 1, MODEL_WIDTH), f32, whole((CHUNKS, 1, MODEL_WIDTH))),
-        *(((2 * dp, *shard.shape), shard.dtype, anywhere) for shard in shards),
+        *(((2 * dp, *shard.shape), shard.dtype, anywhere) for shard in shards[:-1]),
+        ((dp, 2, *shards[-1].shape), shards[-1].dtype, anywhere),
     ]
     pool = (2, 1, MODEL_WIDTH)
     return pl.pallas_call(
@@ -1256,7 +1264,8 @@
             pltpu.VMEM(table.shape, bf16),
             pltpu.SemaphoreType.DMA((2,)),
             *exchange_scratch(line, pool),
-            *gather_sems(line, count),
+            *gather_sems(line, count - 1),
+            *flat_gather_sems(line, 1),
         ],
         compiler_params=pltpu.CompilerParams(
             collective_id=collective_id, has_side_effects=True, vmem_limit_bytes=62 << 20
@@ -1272,7 +1281,7 @@
 
 def backward_kernel(line, count, *refs):
     (
-        proj_ref, probs_ref, upstream_ref, rows_ref, cols_ref, lefts_ref, weight_ref, mixer_grad_ref, normal_ref,
+        proj_ref, probs_ref, upstream_ref, rows_ref, cols_ref, lefts_hbm, weight_ref, mixer_grad_hbm, normal_hbm,
         hits_ref,
     ) = refs[:10]
     ins = refs[10 : 10 + count]
@@ -1282,13 +1291,22 @@
     outs = refs[17 + count : 17 + 2 * count]
     grad_ref, turned_left_ref, input_grad_ref = refs[17 + 2 * count : 20 + 2 * count]
     helpers = refs[20 + 2 * count : 24 + 2 * count]
-    stages = scatter_stages(line, ins, outs, refs[24 + 2 * count :])
+    lefts_ref, mixer_grad_ref, normal_ref, fetch_sem, *rest = refs[24 + 2 * count :]
+    stages = scatter_stages(line, ins, outs, rest)
     step = pl.program_id(0)
+    fetches = [
+        pltpu.make_async_copy(source, target, fetch_sem.at[k])
+        for k, (source, target) in enumerate(
+            ((lefts_hbm, lefts_ref), (mixer_grad_hbm, mixer_grad_ref), (normal_hbm, normal_ref))
+        )
+    ]
 
     @pl.when(step == 0)
     def _():
         greet(line)
         stages.start()
+        for fetch in fetches:
+            fetch.start()
         make_places(rows_ref, cols_ref, *helpers)
         spread(line, 4, 0, 0, stages.first)
 
@@ -1303,12 +1321,9 @@
 
     slots = {
         1: [first(1)],
-        5: [second(0)],
-        6: [first(2)],
-        8: [first(3)],
-        10: [second(1)],
-        15: [third(0)],
-        19: [second(2)],
+        5: [second(0), first(2)],
+        9: [first(3), second(1)],
+        17: [third(0), second(2)],
         21: [second(3)],
     }
 
@@ -1322,6 +1337,12 @@
     @pl.when(jnp.logical_and(step >= PAIRS, step < TABLE_STEP))
     def _():
         column = step - PAIRS
+
+        @pl.when(column == 0)
+        def _():
+            for fetch in fetches:
+                fetch.wait()
+
         source = source_of(column)
         fresh = jnp.logical_or(column == 0, source != source_of(jnp.maximum(column - 1, 0)))
         grads = grad_ref[:, pl.ds(pl.multiple_of(column * MODEL_WIDTH, MODEL_WIDTH), MODEL_WIDTH)]
@@ -1397,10 +1418,10 @@
             pl.BlockSpec((PAGE_TOKENS, LANES), lambda i: (0, pair_at(i))),
             once(anchor_rows.shape),
             once(anchor_cols.shape),
-            once(lefts.shape),
+            anywhere,
             pl.BlockSpec((MODEL_WIDTH, MODEL_WIDTH), lambda i: (0, column_at(i))),
-            once(page),
-            once(page),
+            anywhere,
+            anywhere,
             once(hits.shape),
             *[anywhere] * count,
         ],
@@ -1432,6 +1453,10 @@
             pltpu.VMEM((2, 128, PAGE_TOKENS), jnp.bfloat16),
             pltpu.VMEM((2, 4, PAGE_TOKENS, PAGE_TOKENS), jnp.bfloat16),
             pltpu.VMEM((PAGE_TOKENS, PAGE_TOKENS), jnp.bfloat16),
+            pltpu.VMEM(lefts.shape, jnp.bfloat16),
+            pltpu.VMEM(page, jnp.float32),
+            pltpu.VMEM(page, jnp.float32),
+            pltpu.SemaphoreType.DMA((3,)),
             *scatter_scratch(line, blocks),
         ],
         compiler_params=pltpu.CompilerParams(
@@ -1590,14 +1615,18 @@
     )
 
 
-def finish_kernel(count, share, expand_share, bias_rows, *refs):
-    ins = refs[:count]
-    small_ref, total_ref = refs[count : count + 2]
-    outs = refs[count + 2 : 2 * count + 2]
-    small_outs = refs[2 * count + 2 : 2 * count + 14]
-    staged = refs[2 * count + 14 : 2 * count + 26]
-    sems, small_sems = refs[2 * count + 26 :]
-    copies = [pltpu.make_async_copy(ins[k], outs[k], sems.at[k]) for k in range(count)]
+def finish_kernel(pieces, share, expand_share, bias_rows, *refs):
+    given = pieces[-1][0] + 1
+    count = len(pieces)
+    ins = refs[:given]
+    small_ref, total_ref = refs[given : given + 2]
+    refs = refs[given + 2 :]
+    outs, small_outs, staged = refs[:count], refs[count : count + 12], refs[count + 12 : count + 24]
+    sems, small_sems = refs[count + 24 :]
+    copies = [
+        pltpu.make_async_copy(ins[k].at[:, pl.ds(start, width)], outs[place], sems.at[place])
+        for place, (k, start, width) in enumerate(pieces)
+    ]
     for copy in copies:
         copy.start()
     staged[0][...] = small_ref[:bias_rows, :HEADS]
@@ -1622,17 +1651,21 @@
         copy.wait()
 
 
-def finish(arrays, small, totals, share, expand_share, bias_rows):
-    count = len(arrays)
+def finish(arrays, cut, small, totals, share, expand_share, bias_rows):
+    pieces = [(k, 0, array.shape[1]) for k, array in enumerate(arrays)]
+    if cut:
+        k, start, width = pieces.pop()
+        pieces += [(k, 0, cut), (k, cut, width - cut)]
+    count = len(pieces)
     anywhere = pl.BlockSpec(memory_space=pl.ANY)
     vmem = pl.BlockSpec(memory_space=pltpu.VMEM)
     shapes = [(bias_rows, HEADS)] * 2 + [(1, share)] * 7 + [(1, expand_share)] + [(1, share)] * 2
     return pl.pallas_call(
-        partial(finish_kernel, count, share, expand_share, bias_rows),
-        in_specs=[vmem] * (count + 2),
+        partial(finish_kernel, tuple(pieces), share, expand_share, bias_rows),
+        in_specs=[vmem] * (len(arrays) + 2),
         out_specs=[anywhere] * (count + 12),
         out_shape=[
-            *(jax.ShapeDtypeStruct(array.shape, array.dtype) for array in arrays),
+            *(jax.ShapeDtypeStruct((arrays[k].shape[0], width), jnp.float32) for k, start, width in pieces),
             *(jax.ShapeDtypeStruct(shape, jnp.float32) for shape in shapes),
         ],
         scratch_shapes=[
@@ -1663,11 +1696,10 @@
 
 
 def mixer_kernel(
-    merged_ref, start_ref, cotangent_ref, vectors_ref, bias_ref, merge_ref, expand_ref, reduce_ref,
-    output_ref, mixer_grad_ref, merged_grad_ref, merge_grad_ref, expand_grad_ref, reduce_grad_ref, sums_ref,
-    bias_grad_ref,
+    merged_ref, start_ref, cotangent_ref, vectors_ref, bias_ref, merge_ref, expand_hbm, reduce_hbm,
+    output_ref, mixer_grad_ref, merged_grad_ref, wide_grad_ref, reduce_grad_ref, sums_ref, bias_grad_ref,
     hidden_ref, normal_ref, inverse_ref, low_ref, active_ref, slope_ref, dense_ref, grad_ref, grad_low_ref,
-    turned_ref,
+    turned_ref, expand_ref, reduce_ref, fetch_sem,
 ):
     step = pl.program_id(0)
     chunk = lax.rem(step, CHUNKS)
@@ -1680,8 +1712,15 @@
     def column_sum(values):
         return jnp.sum(values, axis=0, keepdims=True)
 
+    fetches = [
+        pltpu.make_async_copy(source, target, fetch_sem.at[k])
+        for k, (source, target) in enumerate(((expand_hbm, expand_ref), (reduce_hbm, reduce_ref)))
+    ]
+
     @pl.when(step == 0)
     def _():
+        for fetch in fetches:
+            fetch.start()
         normal, inverse = normal_parts(start_ref[...] + dot_nn(merged_ref[...], merge_ref[...]))
         normal_ref[...] = normal
         inverse_ref[...] = jnp.broadcast_to(inverse, inverse_ref.shape)
@@ -1689,6 +1728,8 @@
         hidden_ref[...] = hidden
         low_ref[...] = hidden.astype(jnp.bfloat16)
         dense_ref[...] = jnp.zeros_like(dense_ref)
+        for fetch in fetches:
+            fetch.wait()
 
     @pl.when(step < CHUNKS)
     def _():
@@ -1712,16 +1753,16 @@
         sums_ref[4:5, :] = column_sum(upstream)
         turned_ref[...] = low_ref[...].T
 
-    @pl.when(step >= CHUNKS)
+    @pl.when(jnp.logical_and(step >= CHUNKS, step < 2 * CHUNKS))
     def _():
         grad_low = grad_low_ref[...]
         reduce_grad_ref[...] = dot_tn(active_ref[chunk], grad_low).astype(jnp.bfloat16)
         inner_low = (dot_nt(grad_low, reduce_ref[part, :]) * slope_ref[chunk]).astype(jnp.bfloat16)
         bias_grad_ref[chunk] = column_sum(inner_low.astype(jnp.float32))
-        expand_grad_ref[...] = dot_nn(turned_ref[...], inner_low).astype(jnp.bfloat16)
+        wide_grad_ref[...] = dot_nn(turned_ref[...], inner_low).astype(jnp.bfloat16)
         grad_ref[...] += dot_nt(inner_low, expand_ref[:, part])
 
-    @pl.when(step == 2 * CHUNKS - 1)
+    @pl.when(step == 2 * CHUNKS)
     def _():
         grad = grad_ref[...]
         normal = normal_ref[...]
@@ -1730,7 +1771,7 @@
         sums_ref[0:1, :] = column_sum(grad * normal)
         sums_ref[1:2, :] = column_sum(grad)
         low = mixer_grad.astype(jnp.bfloat16)
-        merge_grad_ref[...] = dot_tn(merged_ref[...], low).astype(jnp.bfloat16)
+        wide_grad_ref[...] = dot_tn(merged_ref[...], low).astype(jnp.bfloat16)
         merged_grad_ref[...] = dot_nt(low, merge_ref[...]).astype(jnp.bfloat16)
 
 
@@ -1741,7 +1782,7 @@
     page = (rows, MODEL_WIDTH)
 
     def back_at(i):
-        return jnp.maximum(i - CHUNKS, 0)
+        return jnp.clip(i - CHUNKS, 0, CHUNKS - 1)
 
     def whole(shape):
         return pl.BlockSpec(shape, lambda i: (0,) * len(shape))
@@ -1751,15 +1792,17 @@
         (page, bf16, whole(page)),
         (page, f32, whole(page)),
         (page, bf16, whole(page)),
-        ((MODEL_WIDTH, MODEL_WIDTH), bf16, whole((MODEL_WIDTH, MODEL_WIDTH))),
-        ((MODEL_WIDTH, inner), bf16, pl.BlockSpec((MODEL_WIDTH, width), lambda i: (0, back_at(i)))),
+        (
+            (MODEL_WIDTH, inner + MODEL_WIDTH), bf16,
+            pl.BlockSpec((MODEL_WIDTH, width), lambda i: (0, jnp.maximum(i - CHUNKS, 0))),
+        ),
         ((inner, MODEL_WIDTH), bf16, pl.BlockSpec((width, MODEL_WIDTH), lambda i: (back_at(i), 0))),
         ((8, MODEL_WIDTH), f32, whole((8, MODEL_WIDTH))),
         ((CHUNKS, 1, width), f32, whole((CHUNKS, 1, width))),
     ]
     return pl.pallas_call(
         mixer_kernel,
-        grid=(2 * CHUNKS,),
+        grid=(2 * CHUNKS + 1,),
         in_specs=[
             once(page),
             once(page),
@@ -1767,8 +1810,8 @@
             once(vectors.shape),
             once(bias.shape),
             once(w_merge.shape),
-            once(w_expand.shape),
-            once(w_reduce.shape),
+            pl.BlockSpec(memory_space=pl.ANY),
+            pl.BlockSpec(memory_space=pl.ANY),
         ],
         out_specs=[spec for shape, kind, spec in outs],
         out_shape=[jax.ShapeDtypeStruct(shape, kind) for shape, kind, spec in outs],
@@ -1783,6 +1826,9 @@
             pltpu.VMEM(page, f32),
             pltpu.VMEM(page, bf16),
             pltpu.VMEM((MODEL_WIDTH, rows), bf16),
+            pltpu.VMEM(w_expand.shape, bf16),
+            pltpu.VMEM(w_reduce.shape, bf16),
+            pltpu.SemaphoreType.DMA((2,)),
         ],
         compiler_params=pltpu.CompilerParams(vmem_limit_bytes=62 << 20),
         name="mixer_layer",
@@ -1858,17 +1904,16 @@
     hits = jnp.stack([text_masked, region_masked], axis=1)
     proj, merged_low, probs, lefts, start_sum, normal_feat, batch_scale, w_vectors, w_expand_bias, *wholes = forward_layer(
         region_features, w_backbone, w_table, text_inputs, hits, packed, w_stream, anchor_rows, anchor_cols,
-        (merge_weight, expand_weight, reduce_weight), token_total, 4,
-    )
-    w_merge, w_expand, w_reduce = (whole.reshape(-1, whole.shape[-1]) for whole in wholes)
+        (expand_weight, reduce_weight, merge_weight), token_total, 4,
+    )
+    w_expand, w_reduce, w_merge = (whole.reshape(-1, whole.shape[-1]) for whole in wholes)
     (
-        layer_output, mixer_in_grad, merged_grad, merge_weight_grad, expand_weight_grad, reduce_weight_grad,
-        mixer_sums, expand_bias_grad,
+        layer_output, mixer_in_grad, merged_grad, wide_grad, reduce_weight_grad, mixer_sums, expand_bias_grad,
     ) = mixer_layer(
         merged_low, start_sum, cotangent, w_vectors, w_expand_bias,
         w_merge, w_expand, w_reduce,
     )
-    early = (expand_weight_grad, reduce_weight_grad, merge_weight_grad)
+    early = (reduce_weight_grad, wide_grad)
     (
         linear_sums, planar_sums, stream_weights_grad, position_table_grad, text_gradient, region_kept,
         start_sums, *early_shares,
@@ -1891,13 +1936,21 @@
         [small_grads, blocks_of(stream_weights_grad, devices)], blocks_of(position_table_grad, devices),
         token_total, 1,
     )
-    arrays = (
-        text_gradient, feature_gradient, backbone_weight_grad, table_share, stream_share, *early_shares,
-    )
+    reduce_share, wide_share = early_shares
+    cut = expand_weight.shape[1]
+    wides = [wide_share]
+    if wide_share.shape[1] != wide_grad.shape[1]:
+        wide_share = wide_share.reshape(-1, wide_grad.shape[1])
+        wides, cut = [wide_share[:, :cut], wide_share[:, cut:]], 0
     (
-        text_gradient, feature_gradient, backbone_weight_grad, table_share, stream_share, expand_share_grad,
-        reduce_share_grad, merge_share_grad, linear_grad, planar_grad, *vector_grads,
-    ) = finish(arrays, small, totals, share, expand_share, bias_rows)
+        text_gradient, feature_gradient, backbone_weight_grad, table_share, stream_share, reduce_share_grad,
+        expand_share_grad, merge_share_grad, linear_grad, planar_grad, *vector_grads,
+    ) = finish(
+        [
+            text_gradient, feature_gradient, backbone_weight_grad, table_share, stream_share, reduce_share, *wides,
+        ],
+        cut, small, totals, share, expand_share, bias_rows,
+    )
     vector_grads = [grad.reshape(-1) for grad in vector_grads]
     return (
         layer_output,

time: 319 us -> 317 us (level)
  no operation moved by 1% of the time
where the time goes in v3:
time: 317 us; the launch traced here: 316 us
  Pallas kernels  306 us (97%)
  local copies, waits for them, and re-layouts  4.48 us (1%)
  other arithmetic  4.09 us (1%)
    pallas_call x1, Pallas kernels, last_layer(): pl.pallas_call(partial(last_kernel, line, count, float(token_total)), in_...  83.6 us
    pallas_call x1, Pallas kernels, gather_all(): pl.pallas_call(partial(gather_kernel, line, count, flat), in_specs=[pl.Bl...  75.1 us
    pallas_call x1, Pallas kernels, backward_layer(): pl.pallas_call(partial(backward_kernel, line, count), grid=(TABLE_STEP +...  62.1 us
    pallas_call x1, Pallas kernels, forward_layer(): pl.pallas_call(partial(forward_kernel, line, count, float(token_total)),...  60 us
    pallas_call x1, Pallas kernels, mixer_layer(): pl.pallas_call(mixer_kernel, grid=(2 * CHUNKS + 1,), in_specs=[once(page)...  20.9 us

profile of v3, /device:TPU:8, one launch (start us, length us, event | category | flops | bytes accessed | tf_op | source)
XLA Modules:
  0.0 315.9 jit_solution(9541025839610023739)
XLA Ops:
  0.7 0.7 pad_add_fusion.1
  1.4 0.7 pad_add_fusion.refs_7_.refs_3_
  2.1 0.0 copy-start
  2.1 1.4 convert_add_fusion.refs_0_
  3.5 0.8 copy.68.refs_4_.refs_9_
  4.3 0.8 copy.67
  5.1 75.1 %gather_all.1 = (f32[32,32,128]{2,1,0:T(8,128)}, bf16[32,64,768]{2,1,0:T(8,128)(2,1)}, bf16[32,24,7680]{2,1,0:T(8,128)(2,1)}, bf16[16,2,32,1536]{3,2,1,0:T(8,128)(2,1)}) custom-call(f32[32,128]{1,0:T(8,128)} %convert_add_fusion.refs_0_, bf16[64,768]{1,0:T(8,128)(2,1)} %refs_1_.1, bf16[24,7680]{1,0:T(8,128)(2,1)} %refs_2_.1, bf16[32,1536]{1,0:T(8,128)(2,1)} %refs_3_.2), custom_call_target="tpu_custom_call" | custom-call | tf_op jit(solution)/shard_map/gather_all/pallas_call | solution.py:569
  80.2 0.0 copy-done
  80.2 60.0 %forward_layer.1 = (bf16[256,7680]{1,0:T(8,128)(2,1)}, bf16[256,768]{1,0:T(8,128)(2,1)}, f32[2,12,256,256]{3,2,1,0:T(8,128)}, bf16[4,256,768]{2,1,0:T(8,128)(2,1...) custom-call(bf16[256,2048]{1,0:T(8,128)(2,1)} %refs_4_.1, ...), custom_call_target="tpu_custom_call" | custom-call | tf_op jit(solution)/shard_map/forward_layer/pallas_call | solution.py:1239
  140.2 20.9 %mixer_layer.1 = (bf16[256,768]{1,0:T(8,128)(2,1)}, f32[256,768]{1,0:T(8,128)}, bf16[256,768]{1,0:T(8,128)(2,1)}, bf16[768,3840]{1,0:T(8,128)(2,1)}, bf16[3072,7...) custom-call(bf16[256,768]{1,0:T(8,128)(2,1)} %get-tuple-element.83.merged_ref, ...), custom_call_target="tpu_custom_call" | custom-call | tf_op jit(solution)/shard_map/mixer_layer/pallas_call | solution.py:1803
  161.1 0.0 copy-start.1
  161.1 0.0 copy-start.2
  161.2 62.1 %backward_layer.1 = (f32[12,1,512]{2,1,0:T(1,128)}, f32[12,1,256]{2,1,0:T(1,128)}, bf16[768,7680]{1,0:T(8,128)(2,1)}, bf16[1024,1536]{1,0:T(8,128)(2,1)}, f32[25...) custom-call(bf16[256,7680]{1,0:T(8,128)(2,1)} %get-tuple-element.91.refs_0_, ...), custom_call_target="tpu_custom_call" | custom-call | tf_op jit(solution)/shard_map/backward_layer/pallas_call | solution.py:1412
  223.3 0.7 slice.18
  224.0 0.0 copy-done.1
  224.0 0.0 copy-done.2
  224.1 0.1 reshape.130
  224.2 0.7 copy.85
  224.9 0.2 slice_reduce_fusion
  225.1 0.1 slice_reduce_fusion.1
  225.2 0.1 copy.70
  225.3 0.1 copy.71
  225.4 0.1 maximum_bitcast_fusion
  225.5 0.1 reshape.129
  225.6 0.1 copy.80
  225.7 0.1 copy.81
  225.8 0.8 copy.83
  226.6 0.8 select_maximum_fusion
  227.4 83.6 %last_layer.1 = (f32[256,2048]{1,0:T(8,128)}, f32[2,768]{1,0:T(2,128)}, f32[24,128]{1,0:T(8,128)}, f32[24,7680]{1,0:T(8,128)}, f32[64,768]{1,0:T(8,128)}, /*index=5*/f32[32,1536]{1,0:T(8,128)}) custom-call(f32[8,768]{1,0:T(8,128)} %get-tuple-element.100.refs_0_, f32[256,768]{1,0:T(8,128)} %get-tuple-element.101.refs_1_, ...), custom_call_target="tpu_custom_call" | custom-call | tf_op jit(solution)/shard_map/last_layer/pallas_call | solution.py:1586
  311.1 4.7 %finish.1 = (f32[256,768]{1,0:T(8,128)}, f32[256,2048]{1,0:T(8,128)}, f32[64,768]{1,0:T(8,128)}, f32[32,1536]{1,0:T(8,128)}, f32[24,7680]{1,0:T(8,128)}, /*index...) custom-call(f32[256,768]{1,0:T(8,128)} %get-tuple-element.99.refs_0_, ...), custom_call_target="tpu_custom_call" | custom-call | tf_op jit(solution)/shard_map/finish/pallas_call | solution.py:1663
  (3 shorter events, 0.1 us)
Async XLA Ops:
  2.1 78.1 %copy-start = (s32[4,256]{1,0:T(4,128)}, s32[4,256]{1,0:T(4,128)S(1)}, u32[]{:S(2)}) copy-start(s32[4,256]{1,0:T(4,128)S(1)} %pad_add_fusion.refs_7_.refs_3_) | copy-start | bytes 12292
  161.1 62.9 %copy-start.1 = (f32[8,768]{1,0:T(8,128)S(1)}, f32[8,768]{1,0:T(8,128)}, u32[]{:S(2)}) copy-start(f32[8,768]{1,0:T(8,128)} %get-tuple-element.105) | copy-start | bytes 73732
  161.1 62.9 %copy-start.2 = (f32[4,1,768]{2,1,0:T(1,128)S(1)}, f32[4,1,768]{2,1,0:T(1,128)}, u32[]{:S(2)}) copy-start(f32[4,1,768]{2,1,0:T(1,128)} %get-tuple-element.106) | copy-start | bytes 36868

commit v4 on v3

--- a/solution.py
+++ b/solution.py
@@ -1115,7 +1115,7 @@
         return vectors_ref[k : k + 1, :]
 
     def hit_rows(stream):
-        return jnp.broadcast_to(hits_ref[:, stream : stream + 1] == 1, (rows, MODEL_WIDTH))
+        return jnp.broadcast_to(hits_ref[:, 4 + stream : 5 + stream] == 1, (rows, MODEL_WIDTH))
 
     @pl.when(step == 0)
     def _():
@@ -1379,7 +1379,7 @@
         sums_ref[...] = jnp.zeros_like(sums_ref)
         for stream, out_ref in enumerate((text_grad_ref, region_grad_ref)):
             grad = mixer_grad + input_grad_ref[2 * stream]
-            hit = jnp.broadcast_to(hits_ref[:, stream : stream + 1] == 1, grad.shape)
+            hit = jnp.broadcast_to(hits_ref[:, 4 + stream : 5 + stream] == 1, grad.shape)
             zero = jnp.zeros_like(grad)
             kept = jnp.where(hit, zero, grad)
             out_ref[...] = kept
@@ -1899,9 +1899,11 @@
         whole.reshape(-1, whole.shape[-1]) for whole in (w_backbone, w_table, w_stream)
     )
 
-    anchor_rows = jnp.concatenate([text_anchors, region_anchors], axis=0)
+    anchor_rows = jnp.concatenate(
+        [text_anchors, region_anchors, text_masked[None, :], region_masked[None, :]], axis=0
+    )
     anchor_cols = anchor_rows.T
-    hits = jnp.stack([text_masked, region_masked], axis=1)
+    hits = anchor_cols
     proj, merged_low, probs, lefts, start_sum, normal_feat, batch_scale, w_vectors, w_expand_bias, *wholes = forward_layer(
         region_features, w_backbone, w_table, text_inputs, hits, packed, w_stream, anchor_rows, anchor_cols,
         (expand_weight, reduce_weight, merge_weight), token_total, 4,

time: 317 us -> 316 us (level)
  no operation moved by 1% of the time
where the time goes in v4:
time: 316 us; the launch traced here: 315 us
  Pallas kernels  307 us (97%)
  local copies, waits for them, and re-layouts  3.68 us (1%)
  other arithmetic  3.43 us (1%)
    pallas_call x1, Pallas kernels, last_layer(): pl.pallas_call(partial(last_kernel, line, count, float(token_total)), in_...  83.7 us
    pallas_call x1, Pallas kernels, gather_all(): pl.pallas_call(partial(gather_kernel, line, count, flat), in_specs=[pl.Bl...  75.1 us
    pallas_call x1, Pallas kernels, backward_layer(): pl.pallas_call(partial(backward_kernel, line, count), grid=(TABLE_STEP +...  62.4 us
    pallas_call x1, Pallas kernels, forward_layer(): pl.pallas_call(partial(forward_kernel, line, count, float(token_total)),...  60 us
    pallas_call x1, Pallas kernels, mixer_layer(): pl.pallas_call(mixer_kernel, grid=(2 * CHUNKS + 1,), in_specs=[once(page)...  20.9 us

profile of v4, /device:TPU:8, one launch (start us, length us, event | category | flops | bytes accessed | tf_op | source)
XLA Modules:
  0.0 314.8 jit_solution(12622768964769059188)
XLA Ops:
  0.7 0.7 pad_add_fusion.refs_7_.refs_3_
  1.4 0.0 copy-start
  1.4 1.5 convert_add_fusion.refs_0_
  2.9 0.8 copy.67
  3.7 75.1 %gather_all.1 = (f32[32,32,128]{2,1,0:T(8,128)}, bf16[32,64,768]{2,1,0:T(8,128)(2,1)}, bf16[32,24,7680]{2,1,0:T(8,128)(2,1)}, bf16[16,2,32,1536]{3,2,1,0:T(8,128)(2,1)}) custom-call(f32[32,128]{1,0:T(8,128)} %convert_add_fusion.refs_0_, bf16[64,768]{1,0:T(8,128)(2,1)} %refs_1_.1, bf16[24,7680]{1,0:T(8,128)(2,1)} %refs_2_.1, bf16[32,1536]{1,0:T(8,128)(2,1)} %refs_3_.2), custom_call_target="tpu_custom_call" | custom-call | tf_op jit(solution)/shard_map/gather_all/pallas_call | solution.py:569
  78.8 0.0 copy-done
  78.8 60.0 %forward_layer.1 = (bf16[256,7680]{1,0:T(8,128)(2,1)}, bf16[256,768]{1,0:T(8,128)(2,1)}, f32[2,12,256,256]{3,2,1,0:T(8,128)}, bf16[4,256,768]{2,1,0:T(8,128)(2,1...) custom-call(bf16[256,2048]{1,0:T(8,128)(2,1)} %refs_4_.1, ...), custom_call_target="tpu_custom_call" | custom-call | tf_op jit(solution)/shard_map/forward_layer/pallas_call | solution.py:1239
  138.8 20.9 %mixer_layer.1 = (bf16[256,768]{1,0:T(8,128)(2,1)}, f32[256,768]{1,0:T(8,128)}, bf16[256,768]{1,0:T(8,128)(2,1)}, bf16[768,3840]{1,0:T(8,128)(2,1)}, bf16[3072,7...) custom-call(bf16[256,768]{1,0:T(8,128)(2,1)} %get-tuple-element.83.merged_ref, ...), custom_call_target="tpu_custom_call" | custom-call | tf_op jit(solution)/shard_map/mixer_layer/pallas_call | solution.py:1803
  159.7 0.0 copy-start.1
  159.7 0.0 copy-start.2
  159.7 62.4 %backward_layer.1 = (f32[12,1,512]{2,1,0:T(1,128)}, f32[12,1,256]{2,1,0:T(1,128)}, bf16[768,7680]{1,0:T(8,128)(2,1)}, bf16[1024,1536]{1,0:T(8,128)(2,1)}, f32[25...) custom-call(bf16[256,7680]{1,0:T(8,128)(2,1)} %get-tuple-element.91.refs_0_, ...), custom_call_target="tpu_custom_call" | custom-call | tf_op jit(solution)/shard_map/backward_layer/pallas_call | solution.py:1412
  222.1 0.7 slice.18
  222.8 0.0 copy-done.1
  222.8 0.0 copy-done.2
  222.9 0.1 reshape.130
  223.0 0.7 copy.83
  223.7 0.2 slice_reduce_fusion
  223.9 0.1 slice_reduce_fusion.1
  224.0 0.1 copy.68
  224.1 0.1 copy.69
  224.2 0.1 maximum_bitcast_fusion
  224.3 0.1 reshape.129
  224.4 0.1 copy.78
  224.5 0.1 copy.79
  224.6 0.8 copy.81
  225.4 0.8 select_maximum_fusion
  226.2 83.7 %last_layer.1 = (f32[256,2048]{1,0:T(8,128)}, f32[2,768]{1,0:T(2,128)}, f32[24,128]{1,0:T(8,128)}, f32[24,7680]{1,0:T(8,128)}, f32[64,768]{1,0:T(8,128)}, /*index=5*/f32[32,1536]{1,0:T(8,128)}) custom-call(f32[8,768]{1,0:T(8,128)} %get-tuple-element.100.refs_0_, f32[256,768]{1,0:T(8,128)} %get-tuple-element.101.refs_1_, ...), custom_call_target="tpu_custom_call" | custom-call | tf_op jit(solution)/shard_map/last_layer/pallas_call | solution.py:1586
  309.9 4.7 %finish.1 = (f32[256,768]{1,0:T(8,128)}, f32[256,2048]{1,0:T(8,128)}, f32[64,768]{1,0:T(8,128)}, f32[32,1536]{1,0:T(8,128)}, f32[24,7680]{1,0:T(8,128)}, /*index...) custom-call(f32[256,768]{1,0:T(8,128)} %get-tuple-element.99.refs_0_, ...), custom_call_target="tpu_custom_call" | custom-call | tf_op jit(solution)/shard_map/finish/pallas_call | solution.py:1663
  (3 shorter events, 0.1 us)
Async XLA Ops:
  1.4 77.4 %copy-start = (s32[6,256]{1,0:T(8,128)}, s32[6,256]{1,0:T(8,128)S(1)}, u32[]{:S(2)}) copy-start(s32[6,256]{1,0:T(8,128)S(1)} %pad_add_fusion.refs_7_.refs_3_) | copy-start | bytes 18436
  159.7 63.1 %copy-start.1 = (f32[8,768]{1,0:T(8,128)S(1)}, f32[8,768]{1,0:T(8,128)}, u32[]{:S(2)}) copy-start(f32[8,768]{1,0:T(8,128)} %get-tuple-element.105) | copy-start | bytes 73732
  159.7 63.2 %copy-start.2 = (f32[4,1,768]{2,1,0:T(1,128)S(1)}, f32[4,1,768]{2,1,0:T(1,128)}, u32[]{:S(2)}) copy-start(f32[4,1,768]{2,1,0:T(1,128)} %get-tuple-element.106) | copy-start | bytes 36868
